TPU v7x, 256 devices: a whole 4x4x8 slice. The times are simulated.
256 devices in a mesh: px: 16 (over y_hi, z), py: 16 (over y_lo, x, core).
Axes of the slice: x: 4, y: 4 (y_hi: 2, y_lo: 2; y = y_hi * 2 + y_lo), z: 8, core: 2. Of those that a mesh axis runs over, the one named last changes fastest.
Arguments:
- field: bfloat16 [2, 64, 64, 4096], P(None, 'px', 'py'), may hold values from -6 to 6
- cotangent: bfloat16 [2, 64, 64, 4096], P(None, 'px', 'py'), may hold values from -6 to 6
- taps: bfloat16 [3, 64, 64, 64], replicated, may hold values from -1 to 1.5, as said below
Outputs:
- mapped: bfloat16 [2, 64, 64, 4096], P(None, 'px', 'py')
- grad_field: bfloat16 [2, 64, 64, 4096], P(None, 'px', 'py')
- grad_taps: float32 [3, 64, 64, 64], P(None, 'px', 'py')
Inputs may be any that keep to these rules, and one draw needn't show every extreme that they name: Every diagonal entry taps[a, 0, c, c] lies between 1 and 1.5, and every diagonal entry taps[a, t, c, c] with t >= 1 has magnitude at most 0.4 / 64.
All inputs are finite; a program needn't handle non-finite values.
Results may differ from a plain program's by a relative error of at most 0.018.
Values may be sent and summed in bfloat16 or wider, within the bound.
A program may use at most 64 MiB of HBM per device.

v0:
```python
import math

import jax
import jax.numpy as jnp
from jax import lax
from jax.sharding import PartitionSpec as P

N = 64
C = 64


def dft_tables(row_ids, col_ids, length):
    product = row_ids[:, None] * col_ids[None, :] % length
    angle = product.astype(jnp.float32) * (2.0 * math.pi / length)
    return (jnp.cos(angle), jnp.sin(angle))


def along(values, table, position):
    letters = "abcdef"[: values.ndim]
    target = letters[:position] + "k" + letters[position + 1 :]
    return jnp.einsum(
        letters + ",k" + letters[position] + "->" + target,
        values,
        table,
        preferred_element_type=jnp.float32,
    )


def section(values, position, cos_b, sin_b, turn_sign, factor):
    direct = along(values, cos_b, position)
    crossed = along(values, sin_b, position)
    half = values.shape[-1] // 2
    turned = jnp.concatenate([crossed[..., half:], -crossed[..., :half]], -1)
    return ((direct + turn_sign * turned) * factor).astype(jnp.bfloat16)


def z_forward(values, cos_b, sin_b):
    direct = along(values, cos_b, 3)
    crossed = along(values, sin_b, 3)
    return jnp.concatenate([direct, -crossed], -1).astype(jnp.bfloat16)


def z_inverse(values, cos_b, sin_b, factor):
    half = values.shape[-1] // 2
    real_part = along(values[..., :half], cos_b, 3)
    imag_part = along(values[..., half:], sin_b, 3)
    return ((real_part - imag_part) * factor).astype(jnp.bfloat16)


def spectra(taps_axis, cos_b, sin_b):
    real_w = jnp.einsum("kt,toi->koi", cos_b, taps_axis, preferred_element_type=jnp.float32)
    imag_w = -jnp.einsum("kt,toi->koi", sin_b, taps_axis, preferred_element_type=jnp.float32)
    upper = jnp.concatenate([real_w, -imag_w], 2)
    lower = jnp.concatenate([imag_w, real_w], 2)
    return jnp.concatenate([upper, lower], 1).astype(jnp.bfloat16)


def push(values, matrix, position):
    letters = "abcde"
    return jnp.einsum(
        letters + "," + letters[position] + "fe->abcdf",
        values,
        matrix,
        preferred_element_type=jnp.float32,
    ).astype(jnp.bfloat16)


def pull(values, matrix, position):
    letters = "abcde"
    return jnp.einsum(
        letters + "," + letters[position] + "ef->abcdf",
        values,
        matrix,
        preferred_element_type=jnp.float32,
    ).astype(jnp.bfloat16)


def outer(left, right, position):
    letters = "abcde"
    return jnp.einsum(
        "abcde,abcdf->" + letters[position] + "ef", left, right, preferred_element_type=jnp.float32
    )


def tap_terms(spectral, cos_f, sin_f, split_t, split_o):
    width = spectral.shape[1] // 2
    count = spectral.shape[0]
    real_g = spectral[:, :width, :width] + spectral[:, width:, width:]
    imag_g = spectral[:, :width, width:] - spectral[:, width:, :width]
    cos_r = cos_f.reshape(count, split_t, -1)
    sin_r = sin_f.reshape(count, split_t, -1)
    real_r = real_g.reshape(count, split_o, -1, width)
    imag_r = imag_g.reshape(count, split_o, -1, width)
    highest = lax.Precision.HIGHEST
    return jnp.einsum("kpu,kqvi->pquvi", cos_r, real_r, precision=highest) + jnp.einsum(
        "kpu,kqvi->pquvi", sin_r, imag_r, precision=highest
    )


def log_terms(taps, row_ids, col_ids, length):
    highest = lax.Precision.HIGHEST
    diag_w = jnp.diagonal(taps.astype(jnp.float32), axis1=2, axis2=3)
    cos_full, sin_full = dft_tables(row_ids, row_ids, length)
    real_z = jnp.einsum("kt,atc->akc", cos_full, diag_w, precision=highest)
    imag_z = -jnp.einsum("kt,atc->akc", sin_full, diag_w, precision=highest)
    modulus = real_z * real_z + imag_z * imag_z
    cos_cols, sin_cols = dft_tables(row_ids, col_ids, length)
    summed = jnp.einsum("kt,akc->atc", cos_cols, real_z / modulus, precision=highest) - jnp.einsum(
        "kt,akc->atc", sin_cols, imag_z / modulus, precision=highest
    )
    return summed / math.sqrt(length)


def per_device(field, cotangent, taps):
    batch_rows = field.shape[0]
    local_x = field.shape[1]
    local_y = field.shape[2]
    count_px = lax.axis_size("px")
    count_py = lax.axis_size("py")
    all_ids = jnp.arange(N, dtype=jnp.int32)
    cos_f, sin_f = dft_tables(all_ids, all_ids, N)
    cos_b = cos_f.astype(jnp.bfloat16)
    sin_b = sin_f.astype(jnp.bfloat16)
    stacked = jnp.concatenate([field, cotangent], 0).reshape(2 * batch_rows, local_x, local_y, N, C)
    spectral = z_forward(stacked, cos_b, sin_b)
    spectral = section(
        lax.all_to_all(spectral, "py", split_axis=3, concat_axis=2, tiled=True),
        2,
        cos_b,
        sin_b,
        1.0,
        1.0,
    )
    spectral = section(
        lax.all_to_all(spectral, "px", split_axis=2, concat_axis=1, tiled=True),
        1,
        cos_b,
        sin_b,
        1.0,
        1.0,
    )
    field_hat = spectral[:batch_rows]
    cot_hat = spectral[batch_rows:]
    count_ky = N // count_px
    count_kz = N // count_py
    ky_ids = lax.axis_index("px") * count_ky + jnp.arange(count_ky, dtype=jnp.int32)
    kz_ids = lax.axis_index("py") * count_kz + jnp.arange(count_kz, dtype=jnp.int32)
    cos_y, sin_y = dft_tables(ky_ids, all_ids, N)
    cos_z, sin_z = dft_tables(kz_ids, all_ids, N)
    lower_mask = jnp.tril(jnp.ones((C, C), jnp.float32))
    masked = (taps.astype(jnp.float32) * lower_mask).astype(jnp.bfloat16)
    mix_x = spectra(masked[0], cos_b, sin_b)
    mix_y = spectra(masked[1], cos_y.astype(jnp.bfloat16), sin_y.astype(jnp.bfloat16))
    mix_z = spectra(masked[2], cos_z.astype(jnp.bfloat16), sin_z.astype(jnp.bfloat16))
    first = push(field_hat, mix_z, 3)
    second = push(first, mix_y, 2)
    out_hat = push(second, mix_x, 1)
    back_two = pull(cot_hat, mix_x, 1)
    back_one = pull(back_two, mix_y, 2)
    back_hat = pull(back_one, mix_z, 3)
    grad_x_spec = outer(cot_hat, second, 1)
    grad_y_spec = outer(back_two, first, 2)
    grad_z_spec = outer(back_one, field_hat, 3)
    returned = section(jnp.concatenate([out_hat, back_hat], 0), 1, cos_b, sin_b, -1.0, 1.0 / N)
    returned = section(
        lax.all_to_all(returned, "px", split_axis=1, concat_axis=2, tiled=True),
        2,
        cos_b,
        sin_b,
        -1.0,
        1.0 / N,
    )
    returned = z_inverse(
        lax.all_to_all(returned, "py", split_axis=2, concat_axis=3, tiled=True),
        cos_b,
        sin_b,
        1.0 / N,
    )
    returned = returned.reshape(2 * batch_rows, local_x, local_y, N * C)
    mapped = returned[:batch_rows]
    grad_field = returned[batch_rows:]
    data_scale = 1.0 / (float(N) ** 4 * math.sqrt(N))
    slab_t = N // count_px
    slab_o = C // count_py
    t_ids = lax.axis_index("px") * slab_t + jnp.arange(slab_t, dtype=jnp.int32)
    o_ids = lax.axis_index("py") * slab_o + jnp.arange(slab_o, dtype=jnp.int32)
    terms = (
        jnp.stack(
            [
                tap_terms(grad_x_spec, cos_f, sin_f, 1, 1),
                tap_terms(grad_y_spec, cos_y, sin_y, 1, 1),
                tap_terms(grad_z_spec, cos_z, sin_z, 1, 1),
            ],
            2,
        )
        * data_scale
    ).reshape(3, N, C, C)
    summed = lax.psum_scatter(
        terms.astype(jnp.bfloat16), "px", scatter_dimension=1, tiled=True
    ).astype(jnp.float32)
    summed = lax.psum_scatter(
        summed.astype(jnp.bfloat16), "py", scatter_dimension=2, tiled=True
    ).astype(jnp.float32)
    log_part = log_terms(taps, all_ids, t_ids, N)
    channel_ids = jnp.arange(C, dtype=jnp.int32)
    diagonal_sel = (channel_ids[None, :] == o_ids[:, None]).astype(jnp.float32)
    keep_mask = (channel_ids[None, :] <= o_ids[:, None]).astype(jnp.float32)
    grad_taps = keep_mask * (summed - log_part[:, :, None, :] * diagonal_sel)
    return (mapped, grad_field, grad_taps)


def solution(mesh):
    return jax.shard_map(
        per_device,
        mesh=mesh,
        in_specs=(P(None, "px", "py", None), P(None, "px", "py", None), P()),
        out_specs=(P(None, "px", "py", None), P(None, "px", "py", None), P(None, "px", "py", None)),
        check_vma=False,
    )
```

profile of v0, /device:TPU:1, one launch (start us, length us, event | category | flops | bytes accessed | tf_op | source)
XLA Modules:
  0.0 469.8 jit_solution(14858885788075312877)
XLA Ops:
  7.2 1.4 pad_maximum_fusion.2
  8.5 0.8 reshape.274
  9.3 0.5 fusion.20
  9.9 0.5 fusion.19
  10.4 0.6 pad_maximum_fusion
  11.0 1.8 copy.82
  12.8 7.3 %all-to-all-start = ((bf16[4,4,4,64,128]{4,2,1,0,3:T(4,128)(2,1)}), bf16[4,4,4,64,128]{4,2,1,0,3:T(4,128)(2,1)}, u32[]{:S(2)}, u32[]{:S(2)}) async-start(bf16[4,4,4,64,128]{4,2,1,0,3:T(4,128)(2,1)} %copy.82), calls=%async_computation | async-start | bytes 2097152 | tf_op jit(solution)/shard_map/all_to_all | solution.py:127
  20.1 4.1 multiply_convert_fusion
  24.2 12.0 %all-to-all-done = bf16[4,4,4,64,128]{4,2,1,0,3:T(4,128)(2,1)} async-done(((bf16[4,4,4,64,128]{4,2,1,0,3:T(4,128)(2,1)}), bf16[4,4,4,64,128]{4,2,1,0,3:T(4,128)(2,1)}, u32[]{:S(2)}, u32[]{:S(2)}) %all-to-all-start) | async-done | bytes 1048608 | tf_op jit(solution)/shard_map/all_to_all | solution.py:127
  36.2 1.8 copy.83
  38.0 0.5 convolution_bitcast_fusion.4
  38.5 0.9 fusion.278
  39.4 0.8 fusion.1
  40.2 1.8 copy.84
  42.0 10.6 %all-to-all-start.1 = ((bf16[4,4,64,4,128]{4,3,1,0,2:T(4,128)(2,1)}), bf16[4,4,64,4,128]{4,3,1,0,2:T(4,128)(2,1)}, u32[]{:S(2)}, u32[]{:S(2)}) async-start(bf16[4,4,64,4,128]{4,3,1,0,2:T(4,128)(2,1)} %copy.84), calls=%async_computation.1 | async-start | bytes 2097152 | tf_op jit(solution)/shard_map/all_to_all | solution.py:135
  54.3 0.5 convolution_convert_fusion.1
  54.9 0.5 fusion.279
  55.4 1.2 maximum_bitcast_fusion
  56.6 22.4 %all-to-all-done.1 = bf16[4,4,64,4,128]{4,3,1,0,2:T(4,128)(2,1)} async-done(((bf16[4,4,64,4,128]{4,3,1,0,2:T(4,128)(2,1)}), bf16[4,4,64,4,128]{4,3,1,0,2:T(4,128)(2,1)}, u32[]{:S(2)}, u32[]{:S(2)}) %all-to-all-start.1) | async-done | bytes 1048608 | tf_op jit(solution)/shard_map/all_to_all | solution.py:135
  79.0 1.8 copy.85
  80.8 0.5 convolution_bitcast_fusion.3
  81.4 0.9 fusion.277
  82.2 0.8 fusion.2
  83.1 1.9 fusion.28
  86.6 0.4 convolution_bitcast_fusion.6
  87.1 2.1 fusion.31
  89.2 3.4 convolution_bitcast_fusion
  93.0 0.7 pad_maximum_fusion.1
  93.7 1.0 convolution_bitcast_fusion.2
  94.6 0.9 fusion.276
  95.5 1.5 fusion.5
  97.0 1.9 copy.101
  98.9 6.3 %all-to-all-start.2 = ((bf16[4,64,4,4,128]{4,3,2,0,1:T(4,128)(2,1)}), bf16[4,64,4,4,128]{4,3,2,0,1:T(4,128)(2,1)}, u32[]{:S(2)}, u32[]{:S(2)}) async-start(bf16[4,64,4,4,128]{4,3,2,0,1:T(4,128)(2,1)} %copy.101), calls=%async_computation.2 | async-start | bytes 2097152 | tf_op jit(solution)/shard_map/all_to_all | solution.py:166
  105.4 3.5 fusion.59
  109.0 3.5 fusion.62
  112.5 3.5 add_bitcast_fusion
  116.0 3.9 add_bitcast_fusion.1
  119.9 1.1 slice_add_fusion
  121.0 4.4 fusion.9
  125.5 4.6 add_bitcast_fusion.2
  130.1 1.0 fusion
  131.1 3.8 copy.116
  134.9 1.9 copy-done.1
  136.7 5.4 %copy.118 = bf16[3,64,64,64]{1,0,3,2:T(4,128)(2,1)} copy(bf16[3,64,64,64]{3,2,1,0:T(8,128)(2,1)S(1)} %copy-done.1) | data formatting | bytes 3145728 | tf_op args[2]
  142.1 0.6 dynamic-slice
  143.4 1.8 copy.102
  145.3 0.5 convolution_bitcast_fusion.1
  145.8 0.9 fusion.275
  146.7 0.8 fusion.8
  147.4 1.9 copy.103
  149.3 4.2 all-to-all-start.3
  153.6 3.0 gather_fusion
  157.6 0.4 fusion.38
  158.0 11.5 %all-to-all-done.3 = bf16[4,4,64,4,128]{4,3,1,0,2:T(4,128)(2,1)S(1)} async-done(((bf16[4,4,64,4,128]{4,3,1,0,2:T(4,128)(2,1)}), bf16[4,4,64,4,128]{4,3,1,0,2:T(4,128)(2,1)S(1)}, u32[]{:S(2)}, u32[]{:S(2)}) %all-to-all-start.3) | async-done | bytes 1048608 | tf_op jit(solution)/shard_map/all_to_all | solution.py:174
  169.5 0.6 copy.104
  170.1 0.5 fusion.40
  170.6 0.7 fusion.21
  171.3 169.2 %reduce-scatter.2.cloned.1.call-done = bf16[3,4,64,64]{3,2,0,1:T(8,128)(2,1)} async-done(((bf16[3,64,64,64]{3,2,0,1:T(8,128)(2,1)}), bf16[3,4,64,64]{3,2,0,1:T(8,128)(2,1)}) %reduce-scatter.2.cloned.1.call-update) | async-done | bytes 98320 | tf_op jit(solution)/shard_map/reduce_scatter | solution.py:198
  340.5 1.8 copy.117
  342.4 1.1 slice.109
  343.5 1.1 slice.111
  344.5 116.9 %all-reduce.3.cloned.1.call-done = bf16[3,4,64,64]{3,1,0,2:T(4,128)(2,1)} async-done(((bf16[3,4,64,64]{3,1,0,2:T(4,128)(2,1)}), bf16[3,4,64,64]{3,1,0,2:T(4,128)(2,1)}) %all-reduce.3.cloned.1.call-update) | async-done | bytes 98320
  461.5 0.7 subtract_multiply_fusion
  462.2 0.6 copy.123
  (34 shorter events, 5.4 us)
Async XLA Ops:
  12.8 23.4 %all-to-all-start = ((bf16[4,4,4,64,128]{4,2,1,0,3:T(4,128)(2,1)}), bf16[4,4,4,64,128]{4,2,1,0,3:T(4,128)(2,1)}, u32[]{:S(2)}, u32[]{:S(2)}) async-start(bf16[4,4,4,64,128]{4,2,1,0,3:T(4,128)(2,1)} %copy.82), calls=%async_computation | async-start | bytes 2097152 | tf_op jit(solution)/shard_map/all_to_all | solution.py:127
  42.0 37.1 %all-to-all-start.1 = ((bf16[4,4,64,4,128]{4,3,1,0,2:T(4,128)(2,1)}), bf16[4,4,64,4,128]{4,3,1,0,2:T(4,128)(2,1)}, u32[]{:S(2)}, u32[]{:S(2)}) async-start(bf16[4,4,64,4,128]{4,3,1,0,2:T(4,128)(2,1)} %copy.84), calls=%async_computation.1 | async-start | bytes 2097152 | tf_op jit(solution)/shard_map/all_to_all | solution.py:135
  98.9 44.6 %all-to-all-start.2 = ((bf16[4,64,4,4,128]{4,3,2,0,1:T(4,128)(2,1)}), bf16[4,64,4,4,128]{4,3,2,0,1:T(4,128)(2,1)}, u32[]{:S(2)}, u32[]{:S(2)}) async-start(bf16[4,64,4,4,128]{4,3,2,0,1:T(4,128)(2,1)} %copy.101), calls=%async_computation.2 | async-start | bytes 2097152 | tf_op jit(solution)/shard_map/all_to_all | solution.py:166
  105.2 235.3 %reduce-scatter.2.cloned.1.call-start = ((), (), s32[]{:S(2)}) async-start(), calls=%async_computation.5 | async-start | bytes 3342336 | tf_op jit(solution)/shard_map/reduce_scatter | solution.py:198
  116.0 3.9 copy-start
  134.8 1.9 copy-start.1
  136.7 5.4 %copy-start.2 = (u32[256]{0:T(256)S(1)}, u32[256]{0:T(256)}, u32[]{:S(2)}) copy-start(u32[256]{0:T(256)} %constant.97) | copy-start | bytes 3076
  149.3 20.2 %all-to-all-start.3 = ((bf16[4,4,64,4,128]{4,3,1,0,2:T(4,128)(2,1)}), bf16[4,4,64,4,128]{4,3,1,0,2:T(4,128)(2,1)S(1)}, u32[]{:S(2)}, u32[]{:S(2)}) async-start(bf16[4,4,64,4,128]{4,3,1,0,2:T(4,128)(2,1)} %copy.103), calls=%async_computation.3 | async-start | bytes 2097152 | tf_op jit(solution)/shard_map/all_to_all | solution.py:174
  153.5 307.9 %all-reduce.3.cloned.1.call-start = ((), (), s32[]{:S(2)}) async-start(), calls=%async_computation.6 | async-start | bytes 393216
Sparse Core Ops, SparseCore 0:
  135.0 205.4 reduce-scatter.1
  343.3 118.1 all-reduce.2
where the time goes:
time: 478 us; the launch traced here: 470 us
  waiting for transfers between devices  332 us (69%)
  matrix products  45.5 us (10%)
  local copies, waits for them, and re-layouts  33.8 us (7%)
  starting transfers between devices  28.5 us (6%)
  between operations  15.3 us (3%)
  other arithmetic  14.8 us (3%)
    reduce_scatter x1, waiting for transfers between devices, per_device(): lax.psum_scatter(terms.astype(jnp.bfloat16), 'px', scatter_dimension=1, t...  169 us
    unnamed x3, waiting for transfers between devices  117 us
    all_to_all x1, waiting for transfers between devices, per_device(): lax.all_to_all(spectral, 'px', split_axis=2, concat_axis=1, tiled=True)  22.4 us
    all_to_all x1, waiting for transfers between devices, per_device(): lax.all_to_all(spectral, 'py', split_axis=3, concat_axis=2, tiled=True)  12 us
    dot_general x3, matrix products, tap_terms(): jnp.einsum('kpu,kqvi->pquvi', sin_r, imag_r, precision=highest)  11.8 us
    dot_general x3, matrix products, tap_terms(): jnp.einsum('kpu,kqvi->pquvi', cos_r, real_r, precision=highest)  11.5 us
    all_to_all x1, waiting for transfers between devices, per_device(): lax.all_to_all(returned, 'py', split_axis=2, concat_axis=3, tiled=True)  11.5 us
    all_to_all x1, starting transfers between devices, per_device(): lax.all_to_all(spectral, 'px', split_axis=2, concat_axis=1, tiled=True)  10.6 us
  transfers between devices with their start and end apart: 6, of which 5 were waited for; matrix products, arithmetic and copies ran while one was open for 12% of the time, Pallas kernels for 0%

commit v1 on v0

v1 whole, which is shorter than its diff:
```python
import math

import jax
import jax.numpy as jnp
import numpy as np
from jax import lax
from jax.experimental import pallas as pl
from jax.experimental.pallas import tpu as pltpu
from jax.sharding import PartitionSpec as P

N = 64
C = 64
PARTS = 16
MESH = pl.DeviceIdType.MESH
F32 = jnp.float32
BF16 = jnp.bfloat16


def lane_sign(shape, dtype=F32):
    lane = lax.broadcasted_iota(jnp.int32, shape, len(shape) - 1)
    return jnp.where(lane < 64, 1.0, -1.0).astype(dtype)


def is_left(shape):
    return lax.broadcasted_iota(jnp.int32, shape, len(shape) - 1) < 64


def swap_halves(x):
    return pltpu.roll(x, 64, x.ndim - 1)


def fft8(xs, turn):
    root = math.sqrt(0.5)

    def turned(v):
        return swap_halves(v) * turn

    def fft4(a0, a1, a2, a3):
        e0, e1, o0, o1 = a0 + a2, a0 - a2, a1 + a3, turned(a1 - a3)
        return (e0 + o0, e1 + o1, e0 - o0, e1 - o1)

    a = [xs[j] + xs[j + 4] for j in range(4)]
    b = [xs[j] - xs[j + 4] for j in range(4)]
    b1 = (b[1] + turned(b[1])) * root
    b2 = turned(b[2])
    b3 = (turned(b[3]) - b[3]) * root
    even = fft4(*a)
    odd = fft4(b[0], b1, b2, b3)
    return [(even, odd)[k % 2][k // 2] for k in range(8)]


def swap_inner(tiles, row4):
    low = row4 < 2
    u = [None] * 4
    for l in range(2):
        u[l] = jnp.where(low, tiles[l], pltpu.roll(tiles[l + 2], 2, 0))
        u[l + 2] = jnp.where(low, pltpu.roll(tiles[l], 6, 0), tiles[l + 2])
    even = row4 % 2 == 0
    v = [None] * 4
    for l in (0, 2):
        v[l] = jnp.where(even, u[l], pltpu.roll(u[l + 1], 1, 0))
        v[l + 1] = jnp.where(even, pltpu.roll(u[l], 7, 0), u[l + 1])
    return v


def swap_pair(first, second, top):
    return (
        jnp.where(top, first, pltpu.roll(second, 4, 0)),
        jnp.where(top, pltpu.roll(first, 4, 0), second),
    )


def layer_kernel(
    field_ref,
    cot_ref,
    taps_ref,
    twc_ref,
    tws_ref,
    cs_ref,
    cosf_ref,
    sinf_ref,
    mapped_ref,
    gfield_ref,
    gtaps_ref,
    taps_v,
    fold,
    mix,
    work,
    hats,
    moves_out,
    moves_in,
    terms,
    grad_out,
    grad_in,
    last_out,
    last_in,
    diag,
    logs,
    taps_sem,
    send_sems,
    recv_sems,
    gsend_sems,
    grecv_sems,
    lsend_sems,
    lrecv_sems,
):
    px = lax.axis_index("px")
    py = lax.axis_index("py")
    same = px == py
    differ = jnp.logical_not(same)

    taps_copy = pltpu.make_async_copy(taps_ref, taps_v, taps_sem)
    taps_copy.start()

    barrier = pltpu.get_barrier_semaphore()

    def greet(i, carry):
        @pl.when(i != py)
        def _():
            pl.semaphore_signal(barrier, inc=1, device_id=(px, i), device_id_type=MESH)

        @pl.when(i != px)
        def _():
            pl.semaphore_signal(barrier, inc=1, device_id=(i, py), device_id_type=MESH)

        @pl.when(jnp.logical_or(differ, i != px))
        def _():
            pl.semaphore_signal(barrier, inc=1, device_id=(py, i), device_id_type=MESH)
            pl.semaphore_signal(barrier, inc=1, device_id=(i, px), device_id_type=MESH)

        return carry

    lax.fori_loop(0, PARTS, greet, 0)

    sgn = lane_sign((1, 128))
    left8 = is_left((8, 128))
    left16 = is_left((16, 128))
    row8 = lax.broadcasted_iota(jnp.int32, (8, 128), 0)
    row4 = row8 % 4
    top = row8 < 4

    def move_route(kind, j):
        if kind == "py":
            return (px, j), py, j == py
        if kind == "px":
            return (j, py), px, j == px
        if kind == "home":
            return (j, px), py, jnp.logical_and(same, j == px)
        return (py, j), px, jnp.logical_and(same, j == py)

    def remote(src, dst, ssem, rsem, device):
        return pltpu.make_async_remote_copy(
            src_ref=src, dst_ref=dst, send_sem=ssem, recv_sem=rsem, device_id=device, device_id_type=MESH
        )

    def start_move(kind, out_at, in_at, ssem, rsem):
        mine = py if kind in ("py", "new") else px

        def step(i, carry):
            j = lax.rem(mine + 1 + i, PARTS)
            device, slot, own = move_route(kind, j)

            @pl.when(own)
            def _():
                in_at(slot)[...] = out_at(j)[...]

            @pl.when(jnp.logical_not(own))
            def _():
                remote(out_at(j), in_at(slot), ssem.at[j], rsem.at[slot], device).start()

            return carry

        lax.fori_loop(0, PARTS, step, 0)

    def own_slot(kind, s):
        if kind == "py":
            return s == py
        if kind == "px":
            return s == px
        return jnp.logical_and(same, s == px)

    def wait_in(kind, in_at, ssem, rsem):
        def step(s, carry):
            @pl.when(jnp.logical_not(own_slot(kind, s)))
            def _():
                remote(in_at(s), in_at(s), ssem.at[s], rsem.at[s], (px, py)).wait_recv()

            return carry

        lax.fori_loop(0, PARTS, step, 0)

    def wait_out(kind, out_at, ssem, rsem):
        def step(j, carry):
            @pl.when(jnp.logical_not(own_slot(kind, j)))
            def _():
                remote(out_at(j), out_at(j), ssem.at[j], rsem.at[j], (px, py)).wait_send()

            return carry

        lax.fori_loop(0, PARTS, step, 0)

    KINDS = ("new", "py", "px", "px", "py", "home")

    def blocks(ref, m):
        return lambda j: ref.at[m, pl.ds(pl.multiple_of(j * 4, 4), 4)]

    def send(m):
        start_move(KINDS[m], blocks(moves_out, m), blocks(moves_in, m), send_sems.at[m], recv_sems.at[m])

    def receive(m):
        wait_in(KINDS[m], blocks(moves_in, m), send_sems.at[m], recv_sems.at[m])

    def unpack(ref):
        def step(j, carry):
            lanes = pl.ds(pl.multiple_of(j * 128, 128), 128)
            a0 = ref[0:16, lanes].astype(F32)
            a1 = ref[16:32, lanes].astype(F32)
            work[2 * j] = jnp.where(left16, a0, swap_halves(a1))
            work[2 * j + 1] = jnp.where(left16, swap_halves(a0), a1)
            return carry

        lax.fori_loop(0, N // 2, step, 0, unroll=4)

    def repack(load, ref):
        def step(j, carry):
            lanes = pl.ds(pl.multiple_of(j * 128, 128), 128)
            a0 = load(2 * j)
            a1 = load(2 * j + 1)
            ref[0:16, lanes] = jnp.where(left16, a0, swap_halves(a1)).astype(BF16)
            ref[16:32, lanes] = jnp.where(left16, swap_halves(a0), a1).astype(BF16)
            return carry

        lax.fori_loop(0, N // 2, step, 0, unroll=4)

    def pack_inner(m):
        def step(g, carry):
            halves = [
                swap_inner([work[4 * g + l, 8 * h : 8 * h + 8, :] for l in range(4)], row4) for h in range(2)
            ]
            for b in range(4):
                moves_out[m, 4 * g + b] = jnp.concatenate([halves[0][b], halves[1][b]], 0).astype(BF16)
            return carry

        lax.fori_loop(0, PARTS, step, 0, unroll=2)

    def pack_outer(m):
        def step(g, carry):
            out = [[None, None] for _ in range(4)]
            for h in range(2):
                for h2 in range(2):
                    rows = slice(8 * h, 8 * h + 8)
                    out[2 * h][h2], out[2 * h + 1][h2] = swap_pair(
                        work[4 * g + 2 * h2, rows, :], work[4 * g + 2 * h2 + 1, rows, :], top
                    )
            for b in range(4):
                moves_out[m, 4 * g + b] = jnp.concatenate(out[b], 0).astype(BF16)
            return carry

        lax.fori_loop(0, PARTS, step, 0, unroll=2)

    def twiddle(v, row, direction):
        cos_row = twc_ref[pl.ds(row, 1), :]
        sin_row = tws_ref[pl.ds(row, 1), :] * direction
        return v * cos_row + swap_halves(v) * sin_row

    def transform_in(load):
        def step(j, carry):
            out = fft8([load(8 * m + j) for m in range(8)], sgn)
            work[j] = out[0]
            for k1 in range(1, 8):
                work[8 * k1 + j] = twiddle(out[k1], 8 * k1 + j, 1.0)
            return carry

        lax.fori_loop(0, 8, step, 0)

    def mix_spectrum(hat, axis, push):
        contract = (((1,), (1 if push else 0,)), ((), ()))

        def step(k1, carry):
            out = fft8([work[8 * k1 + j] for j in range(8)], sgn)
            mixed = []
            for k2 in range(8):
                v = out[k2].astype(BF16)
                hats[hat, k1 + 8 * k2] = v
                mixed.append(
                    lax.dot_general(v, mix[axis, k1 + 8 * k2], contract, preferred_element_type=F32)
                )
            back = fft8(mixed, -sgn)
            for j in range(8):
                work[8 * k1 + j] = twiddle(back[j], 8 * k1 + j, -1.0)
            return carry

        lax.fori_loop(0, 8, step, 0)

    def transform_out():
        def step(j, carry):
            out = fft8([work[8 * k1 + j] for k1 in range(8)], -sgn)
            for m in range(8):
                work[8 * m + j] = out[m]
            return carry

        lax.fori_loop(0, 8, step, 0)

    def arrived(m):
        return lambda n: moves_in[m, n].astype(F32)

    def stage(load, hat, axis, push):
        transform_in(load)
        mix_spectrum(hat, axis, push)
        transform_out()

    def cs_transform(emit):
        def step(k, carry):
            even = fold[0] * cs_ref[0:1, :]
            odd = jnp.zeros((C, 128), F32)
            for t in range(1, 33):
                term = fold[t] * cs_ref[pl.ds(lax.rem(k * t, N), 1), :]
                if t % 2:
                    odd = odd + term
                else:
                    even = even + term
            emit(k, even + odd)
            emit(32 - k, (even - odd) * sgn)
            return carry

        lax.fori_loop(0, 17, step, 0)

    def make_mix(axis):
        row = lax.broadcasted_iota(jnp.int32, (C, C), 0)
        col = lax.broadcasted_iota(jnp.int32, (C, C), 1)

        def step(t, carry):
            later = lax.rem(N - t, N)
            ta = taps_v[axis, t].astype(F32)
            tb = taps_v[axis, later].astype(F32)
            diag[axis, pl.ds(t, 1), :] = jnp.sum(jnp.where(row == col, ta, 0.0), 0, keepdims=True)
            diag[axis, pl.ds(later, 1), :] = jnp.sum(jnp.where(row == col, tb, 0.0), 0, keepdims=True)
            ta = jnp.where(col <= row, ta, 0.0)
            tb = jnp.where(col <= row, tb, 0.0)
            once = jnp.logical_or(t == 0, t == 32)
            both = jnp.where(once, ta, ta + tb)
            fold[t] = jnp.concatenate([both, ta - tb], 1)
            return carry

        lax.fori_loop(0, 33, step, 0)

        def emit(k, a):
            a = a * (1.0 / N)
            flipped = swap_halves(a)
            mix[axis, k] = jnp.concatenate([a, flipped * -sgn], 0).astype(BF16)
            mix[axis, lax.rem(N - k, N)] = jnp.concatenate([a * sgn, flipped], 0).astype(BF16)

        cs_transform(emit)

    def make_logs():
        highest = lax.Precision.HIGHEST

        def dot(a, b):
            return jnp.dot(a, b, precision=highest, preferred_element_type=F32)

        cos_t, sin_t = cosf_ref[...], sinf_ref[...]
        for axis in range(3):
            d = diag[axis]
            real_z, imag_z = dot(cos_t, d), -dot(sin_t, d)
            modulus = real_z * real_z + imag_z * imag_z
            logs[axis] = (dot(cos_t, real_z / modulus) - dot(sin_t, imag_z / modulus)) * (1.0 / math.sqrt(N))

    def grad_terms(axis, cot_hat, field_hat):
        sgn_b = lane_sign((16, 128), BF16)
        contract = (((0,), (0,)), ((), ()))

        def fill(p, v, u):
            g = lax.dot_general(v, u, contract, preferred_element_type=F32)
            fold[p] = g[:C] + swap_halves(g[C:]) * sgn

        fill(0, hats[cot_hat, 0], hats[field_hat, 0])
        fill(32, hats[cot_hat, 32], hats[field_hat, 32])

        def step(p, carry):
            v = jnp.concatenate([hats[cot_hat, p], hats[cot_hat, N - p] * sgn_b], 0)
            u = jnp.concatenate([hats[field_hat, p], hats[field_hat, N - p] * sgn_b], 0)
            fill(p, v, u)
            return carry

        lax.fori_loop(1, 32, step, 0)
        scale = 1.0 / (float(N) ** 2 * math.sqrt(N))

        def emit(t, h):
            h = h * scale
            flipped = swap_halves(h)
            terms[t] = h + flipped
            terms[lax.rem(N - t, N)] = (h - flipped) * sgn

        cs_transform(emit)

        def spread(g, carry):
            for q in range(8):
                rows = slice(8 * q, 8 * q + 8)
                part = [
                    jnp.where(left8, terms[8 * g + 2 * i, rows, :], terms[8 * g + 2 * i + 1, rows, :])
                    for i in range(4)
                ]
                a0, b0 = swap_pair(part[0], part[1], top)
                a1, b1 = swap_pair(part[2], part[3], top)
                grad_out[axis, 2 * q, g] = jnp.concatenate([a0, a1], 0).astype(BF16)
                grad_out[axis, 2 * q + 1, g] = jnp.concatenate([b0, b1], 0).astype(BF16)
            return carry

        lax.fori_loop(0, 8, spread, 0)
        start_move("py", *grad_ends(axis))

    def grad_ends(axis):
        return (
            lambda j: grad_out.at[axis, j],
            lambda j: grad_in.at[axis, j],
            gsend_sems.at[axis],
            grecv_sems.at[axis],
        )

    last_ends = (lambda j: last_out.at[j], lambda j: last_in.at[j], lsend_sems, lrecv_sems)

    unpack(cot_ref)
    pack_inner(0)
    pl.semaphore_wait(barrier, jnp.where(same, 4 * PARTS - 4, 4 * PARTS - 2))
    send(0)
    taps_copy.wait()
    make_mix(2)
    unpack(field_ref)
    stage(lambda n: work[n], 0, 2, True)
    pack_inner(1)
    send(1)

    make_mix(0)
    receive(0)
    stage(arrived(0), 1, 0, False)
    pack_outer(2)
    send(2)

    make_mix(1)
    receive(1)
    stage(arrived(1), 2, 1, True)
    pack_outer(3)
    send(3)

    make_logs()
    receive(2)
    stage(arrived(2), 3, 1, False)
    pack_inner(4)
    send(4)

    receive(3)
    stage(arrived(3), 4, 0, True)
    pack_inner(5)
    send(5)
    grad_terms(1, 3, 2)
    grad_terms(0, 1, 4)

    receive(4)
    stage(arrived(4), 5, 2, False)
    repack(lambda n: work[n], gfield_ref)
    grad_terms(2, 5, 0)
    receive(5)
    repack(arrived(5), mapped_ref)

    for axis in (1, 0, 2):
        start, end, ssem, rsem = grad_ends(axis)
        wait_in("py", end, ssem, rsem)

    def add_up(g, carry):
        sums = []
        for axis in range(3):
            total = grad_in[axis, 0, g].astype(F32)
            for s in range(1, PARTS):
                total = total + grad_in[axis, s, g].astype(F32)
            sums.append(total)
        for h in range(2):
            rows = slice(8 * h, 8 * h + 8)
            parts = [s[rows] for s in sums] + [jnp.zeros((8, 128), F32)]
            last_out[2 * g + h] = jnp.concatenate(parts, 0).astype(BF16)
        return carry

    lax.fori_loop(0, 8, add_up, 0)
    start_move("px", *last_ends)
    wait_in("px", last_ends[1], lsend_sems, lrecv_sems)
    total = last_in[0].astype(F32)
    for s in range(1, PARTS):
        total = total + last_in[s].astype(F32)
    row = lax.broadcasted_iota(jnp.int32, (4, C), 0) + 4 * py
    col = lax.broadcasted_iota(jnp.int32, (4, C), 1)
    for axis in range(3):
        for t in range(4):
            rows = slice(8 * axis + 4 * (t // 2), 8 * axis + 4 * (t // 2) + 4)
            own = total[rows, 64 * (t % 2) : 64 * (t % 2) + 64]
            log_row = logs[axis, pl.ds(4 * px + t, 1), :]
            own = own - jnp.where(row == col, log_row, 0.0)
            gtaps_ref[axis, t] = jnp.where(col <= row, own, 0.0)

    for m in range(6):
        wait_out(KINDS[m], blocks(moves_out, m), send_sems.at[m], recv_sems.at[m])
    for axis in range(3):
        start, end, ssem, rsem = grad_ends(axis)
        wait_out("py", start, ssem, rsem)
    wait_out("px", last_ends[0], lsend_sems, lrecv_sems)


def tables():
    angle = np.arange(N) * (2.0 * np.pi / N)
    cos = np.round(np.cos(angle), 15)
    sin = np.round(np.sin(angle), 15)
    product = np.arange(8)[:, None] * np.arange(8)[None, :]
    flat = product.reshape(-1)
    ones = np.ones((1, 64))
    twc = np.concatenate([cos[flat][:, None] * ones] * 2, 1)
    tws = np.concatenate([sin[flat][:, None] * ones, -sin[flat][:, None] * ones], 1)
    cs = np.concatenate([cos[:, None] * ones, sin[:, None] * ones], 1)
    grid = np.arange(N)[:, None] * np.arange(N)[None, :] % N
    return [np.asarray(a, np.float32) for a in (twc, tws, cs, cos[grid], sin[grid])]


def per_device(field, cotangent, taps):
    rows = field.reshape(32, N * C)
    cot_rows = cotangent.transpose(0, 2, 1, 3).reshape(32, N * C)
    vmem = pl.BlockSpec(memory_space=pltpu.VMEM)
    dma = pltpu.SemaphoreType.DMA
    mapped, gfield, gtaps = pl.pallas_call(
        layer_kernel,
        out_shape=(
            jax.ShapeDtypeStruct((32, N * C), BF16),
            jax.ShapeDtypeStruct((32, N * C), BF16),
            jax.ShapeDtypeStruct((3, 4, 4, C), F32),
        ),
        in_specs=[vmem, vmem, pl.BlockSpec(memory_space=pl.ANY)] + [vmem] * 5,
        out_specs=(vmem, vmem, vmem),
        scratch_shapes=[
            pltpu.VMEM((3, N, C, C), BF16),
            pltpu.VMEM((33, C, 128), F32),
            pltpu.VMEM((3, N, 128, 128), BF16),
            pltpu.VMEM((N, 16, 128), F32),
            pltpu.VMEM((6, N, 16, 128), BF16),
            pltpu.VMEM((6, N, 16, 128), BF16),
            pltpu.VMEM((6, N, 16, 128), BF16),
            pltpu.VMEM((N, C, 128), F32),
            pltpu.VMEM((3, PARTS, 8, 16, 128), BF16),
            pltpu.VMEM((3, PARTS, 8, 16, 128), BF16),
            pltpu.VMEM((PARTS, 32, 128), BF16),
            pltpu.VMEM((PARTS, 32, 128), BF16),
            pltpu.VMEM((3, N, C), F32),
            pltpu.VMEM((3, N, C), F32),
            dma(()),
            dma((6, PARTS)),
            dma((6, PARTS)),
            dma((3, PARTS)),
            dma((3, PARTS)),
            dma((PARTS,)),
            dma((PARTS,)),
        ],
        compiler_params=pltpu.CompilerParams(
            collective_id=0, has_side_effects=True, vmem_limit_bytes=48 * 1024 * 1024
        ),
        name="flow_layer",
    )(rows, cot_rows, taps, *[jnp.asarray(t) for t in tables()])
    mapped = mapped.reshape(2, 4, 4, N * C).transpose(0, 2, 1, 3)
    return (mapped, gfield.reshape(2, 4, 4, N * C), gtaps)


def solution(mesh):
    return jax.shard_map(
        per_device,
        mesh=mesh,
        in_specs=(P(None, "px", "py", None), P(None, "px", "py", None), P()),
        out_specs=(P(None, "px", "py", None), P(None, "px", "py", None), P(None, "px", "py", None)),
        check_vma=False,
    )
```

time: 478 us -> 145 us (0.30); the launches traced: 470 us -> 144 us
  waiting for transfers between devices: 332 us -> 0 us
  Pallas kernels: 0 us -> 133 us
  matrix products: 45.5 us -> 0 us
  starting transfers between devices: 28.5 us -> 0 us
  local copies, waits for them, and re-layouts: 33.8 us -> 10.3 us
  other arithmetic: 14.8 us -> 0 us
  between operations: 15.3 us -> 0.67 us
    reduce_scatter x1 -> x0, waiting for transfers between devices: 169 us -> none  [per_device(): lax.psum_scatter(terms.astype(jnp.bfloat16), 'px', scatter_dimension=1, t...]
    pallas_call x0 -> x1, Pallas kernels: none -> 133 us  [per_device(): pl.pallas_call(layer_kernel, out_shape=(jax.ShapeDtypeStruct((32, N * C),...]
    unnamed x3 -> x0, waiting for transfers between devices: 117 us -> none
    all_to_all x4 -> x0, waiting for transfers between devices: 45.9 us -> none  [the longest x1 22.4 us: per_device(): lax.all_to_all(spectral, 'px', split_axis=2, concat_axis=1, tiled=True)]
    dot_general x37 -> x0, matrix products: 45.5 us -> none  [the longest x3 11.8 us: tap_terms(): jnp.einsum('kpu,kqvi->pquvi', sin_r, imag_r, precision=highest)]
    all_to_all x4 -> x0, starting transfers between devices: 28.4 us -> none  [the longest x1 10.6 us: per_device(): lax.all_to_all(spectral, 'px', split_axis=2, concat_axis=1, tiled=True)]
    convert_element_type x4 -> x0, local copies, waits for them, and re-layouts: 9.29 us -> none  [the longest x3 5.51 us: section(): return ((direct + turn_sign * turned) * factor).astype(jnp.bfloat16)]
    all_to_all x4 -> x0, local copies, waits for them, and re-layouts: 5.98 us -> none  [the longest x1 1.81 us: per_device(): lax.all_to_all(returned, 'px', split_axis=1, concat_axis=2, tiled=True)]
  transfers between devices with their start and end apart: 6 -> 0, of which waited for: 5 -> 0; matrix products, arithmetic and copies ran while one was open for 12% -> 0% of each run, Pallas kernels for 0% -> 0%
where the time goes in v1:
time: 145 us; the launch traced here: 144 us
  Pallas kernels  133 us (92%)
  local copies, waits for them, and re-layouts  10.3 us (7%)
    pallas_call x1, Pallas kernels, per_device(): pl.pallas_call(layer_kernel, out_shape=(jax.ShapeDtypeStruct((32, N * C),...  133 us
    unnamed x13, local copies, waits for them, and re-layouts  6.28 us

profile of v1, /device:TPU:1, one launch (start us, length us, event | category | flops | bytes accessed | tf_op | source)
XLA Modules:
  0.0 144.3 jit_solution(18349055357756089782)
XLA Ops:
  0.6 1.0 reshape.18.field_ref
  1.6 1.2 copy.11
  2.8 0.1 reshape.19.cot_ref
  2.9 0.0 copy-start
  2.9 1.9 %copy-done = bf16[3,64,64,64]{3,2,1,0:T(8,128)(2,1)S(1)} copy-done((bf16[3,64,64,64]{3,2,1,0:T(8,128)(2,1)S(1)}, bf16[3,64,64,64]{3,2,1,0:T(8,128)(2,1)}, u32[]{:S(2)}) %copy-start) | copy-done | bytes 1572888
  4.8 0.0 copy-start.1
  4.8 0.8 copy-done.1
  5.5 0.0 copy-start.2
  5.5 0.8 copy-done.2
  6.3 0.0 copy-start.3
  6.3 0.8 copy-done.3
  7.0 0.0 copy-start.4
  7.0 0.8 copy-done.4
  7.8 0.0 copy-start.5
  7.8 0.8 copy-done.5
  8.6 133.3 %flow_layer.1 = (bf16[32,4096]{1,0:T(8,128)(2,1)S(1)}, bf16[32,4096]{1,0:T(8,128)(2,1)S(1)}, f32[3,4,4,64]{3,2,1,0:T(4,128)S(1)}) custom-call(bf16[32,4096]{1,0:T(8,128)(2,1)S(1)} %reshape.18.field_ref, bf16[32,4096]{1,0:T(8,128)(2,1)S(1)} %reshape.19.cot_ref, bf16[3,64,64,64]{3,2,1,0:T(8,128)(2,1)S(1)} %copy-done, f32[64,128]{1,0:T(8,128)S(1)} %copy-done.5, ...), custom_call_target="tpu_custom_call" | custom-call | tf_op jit(solution)/shard_map/flow_layer/pallas_call | solution.py:525
  141.9 0.1 reshape.20
  142.0 0.9 copy.14
  142.9 0.8 reshape.21
  143.7 0.6 copy.16
Async XLA Ops:
  2.9 1.9 %copy-start = (bf16[3,64,64,64]{3,2,1,0:T(8,128)(2,1)S(1)}, bf16[3,64,64,64]{3,2,1,0:T(8,128)(2,1)}, u32[]{:S(2)}) copy-start(bf16[3,64,64,64]{3,2,1,0:T(8,128)(2,1)} %taps_ref.1) | copy-start | bytes 4718596
  4.8 0.8 copy-start.1
  5.5 0.8 copy-start.2
  6.3 0.8 copy-start.3
  7.0 0.8 copy-start.4
  7.8 0.8 copy-start.5

commit v2 on v1

v2 whole, which is shorter than its diff:
```python
import math

import jax
import jax.numpy as jnp
from jax import lax
from jax.experimental import pallas as pl
from jax.experimental.pallas import tpu as pltpu
from jax.sharding import PartitionSpec as P

N = 64
C = 64
PARTS = 16
MESH = pl.DeviceIdType.MESH
F32 = jnp.float32
BF16 = jnp.bfloat16


def swap_halves(x):
    return pltpu.roll(x, 64, x.ndim - 1)


def add(a, b):
    return (a[0] + b[0], a[1] + b[1])


def sub(a, b):
    return (a[0] - b[0], a[1] - b[1])


def add_turned(a, b, forward):
    if forward:
        return (a[0] + b[1], a[1] - b[0])
    return (a[0] - b[1], a[1] + b[0])


def fft8(xs, forward):
    root = math.sqrt(0.5)

    def finish(e0, e1, c, d):
        o0, o1 = add(c, d), sub(c, d)
        return (add(e0, o0), add_turned(e1, o1, forward), sub(e0, o0), add_turned(e1, o1, not forward))

    a = [add(xs[j], xs[j + 4]) for j in range(4)]
    b = [sub(xs[j], xs[j + 4]) for j in range(4)]
    b1 = add_turned(b[1], b[1], forward)
    b3 = add_turned(b[3], b[3], not forward)
    b1 = (b1[0] * root, b1[1] * root)
    b3 = (b3[0] * -root, b3[1] * -root)
    even = finish(add(a[0], a[2]), sub(a[0], a[2]), a[1], a[3])
    odd = finish(add_turned(b[0], b[2], forward), add_turned(b[0], b[2], not forward), b1, b3)
    return [(even, odd)[k % 2][k // 2] for k in range(8)]


def swap_inner(tiles, row4):
    low = row4 < 2
    u = [None] * 4
    for l in range(2):
        u[l] = jnp.where(low, tiles[l], pltpu.roll(tiles[l + 2], 2, 0))
        u[l + 2] = jnp.where(low, pltpu.roll(tiles[l], 6, 0), tiles[l + 2])
    even = row4 % 2 == 0
    v = [None] * 4
    for l in (0, 2):
        v[l] = jnp.where(even, u[l], pltpu.roll(u[l + 1], 1, 0))
        v[l + 1] = jnp.where(even, pltpu.roll(u[l], 7, 0), u[l + 1])
    return v


def swap_pair(first, second, top):
    return (
        jnp.where(top, first, pltpu.roll(second, 4, 0)),
        jnp.where(top, pltpu.roll(first, 4, 0), second),
    )


def swap_lanes(first, second, left):
    return (
        jnp.where(left, first, swap_halves(second)),
        jnp.where(left, swap_halves(first), second),
    )


def swap_outer(tiles, top, left):
    u0, u1 = swap_pair(tiles[0], tiles[1], top)
    u2, u3 = swap_pair(tiles[2], tiles[3], top)
    v0, v2 = swap_lanes(u0, u2, left)
    v1, v3 = swap_lanes(u1, u3, left)
    return [v0, v1, v2, v3]


def layer_kernel(
    field_ref,
    cot_ref,
    taps_ref,
    mapped_ref,
    gfield_ref,
    gtaps_ref,
    taps_v,
    tw_cos,
    tw_sin,
    tw_both,
    fold,
    mix,
    work,
    cot_hats,
    field_hats,
    moves_out,
    moves_in,
    terms,
    grad_out,
    grad_in,
    last_out,
    last_in,
    diag,
    logs,
    taps_sem,
    send_sems,
    recv_sems,
    gsend_sems,
    grecv_sems,
    lsend_sems,
    lrecv_sems,
):
    px = lax.axis_index("px")
    py = lax.axis_index("py")
    same = px == py
    differ = jnp.logical_not(same)

    barrier = pltpu.get_barrier_semaphore()

    def greet(i, carry):
        @pl.when(i != px)
        def _():
            pl.semaphore_signal(barrier, inc=1, device_id=(i, py), device_id_type=MESH)

        @pl.when(i != py)
        def _():
            pl.semaphore_signal(barrier, inc=1, device_id=(px, i), device_id_type=MESH)

        @pl.when(jnp.logical_or(differ, i != py))
        def _():
            pl.semaphore_signal(barrier, inc=1, device_id=(py, i), device_id_type=MESH)

        return carry

    lax.fori_loop(0, PARTS, greet, 0)

    taps_copy = pltpu.make_async_copy(taps_ref, taps_v, taps_sem)
    taps_copy.start()

    left = lax.broadcasted_iota(jnp.int32, (8, 128), 1) < 64
    sgn = jnp.where(left, 1.0, -1.0).astype(F32)
    row8 = lax.broadcasted_iota(jnp.int32, (8, 128), 0)
    row4 = row8 % 4
    top = row8 < 4

    def make_tables():
        angle = lax.broadcasted_iota(jnp.int32, (N, 128), 0).astype(F32) * (2.0 * math.pi / N)
        cos, sin = jnp.cos(angle), jnp.sin(angle)
        for r in range(N):
            c = jnp.broadcast_to(cos[r : r + 1, :], (8, 128))
            s = jnp.broadcast_to(sin[r : r + 1, :], (8, 128))
            tw_cos[r] = c
            tw_sin[r] = s
            tw_both[r] = jnp.where(left, c, s)

    def move_route(kind, j):
        if kind == "py":
            return (px, j), py, j == py
        if kind == "px":
            return (j, py), px, j == px
        return (j, px), py, jnp.logical_and(same, j == px)

    def own_slot(kind, s):
        if kind == "py":
            return s == py
        if kind == "px":
            return s == px
        return jnp.logical_and(same, s == px)

    def remote(src, dst, ssem, rsem, device):
        return pltpu.make_async_remote_copy(
            src_ref=src, dst_ref=dst, send_sem=ssem, recv_sem=rsem, device_id=device, device_id_type=MESH
        )

    def start_move(kind, out_at, in_at, ssem, rsem):
        mine = py if kind == "py" else px

        def step(i, carry):
            j = lax.rem(mine + 1 + i, PARTS)
            device, slot, own = move_route(kind, j)

            @pl.when(own)
            def _():
                in_at(slot)[...] = out_at(j)[...]

            @pl.when(jnp.logical_not(own))
            def _():
                remote(out_at(j), in_at(slot), ssem.at[j], rsem.at[slot], device).start()

            return carry

        lax.fori_loop(0, PARTS, step, 0)

    def wait_in_slot(kind, in_at, ssem, rsem, s):
        @pl.when(jnp.logical_not(own_slot(kind, s)))
        def _():
            remote(in_at(s), in_at(s), ssem.at[s], rsem.at[s], (px, py)).wait_recv()

    def wait_in(kind, in_at, ssem, rsem):
        def step(s, carry):
            wait_in_slot(kind, in_at, ssem, rsem, s)
            return carry

        lax.fori_loop(0, PARTS, step, 0)

    def wait_out(kind, out_at, ssem, rsem):
        def step(j, carry):
            @pl.when(jnp.logical_not(own_slot(kind, j)))
            def _():
                remote(out_at(j), out_at(j), ssem.at[j], rsem.at[j], (px, py)).wait_send()

            return carry

        lax.fori_loop(0, PARTS, step, 0)

    KINDS = ("px", "turn", "py", "py", "py", "px", "px")

    def blocks(ref, m):
        return lambda j: ref.at[m, pl.ds(pl.multiple_of(j * 4, 4), 4)]

    def leaving(m):
        return blocks(moves_in, 4) if m == 5 else blocks(moves_out, m)

    def send(m):
        start_move(KINDS[m], leaving(m), blocks(moves_in, m), send_sems.at[m], recv_sems.at[m])

    def receive(m):
        wait_in(KINDS[m], blocks(moves_in, m), send_sems.at[m], recv_sems.at[m])

    def forward():
        def step(i, carry):
            j = lax.rem(py + PARTS - i, PARTS)
            wait_in_slot("py", blocks(moves_in, 4), send_sems.at[4], recv_sems.at[4], j)
            device, slot, own = move_route("px", j)
            source, target = leaving(5)(j), blocks(moves_in, 5)(slot)

            @pl.when(own)
            def _():
                target[...] = source[...]

            @pl.when(jnp.logical_not(own))
            def _():
                remote(source, target, send_sems.at[5, j], recv_sems.at[5, slot], device).start()

            return carry

        lax.fori_loop(0, PARTS, step, 0)

    def unpack(ref):
        def step(i, carry):
            for u in range(2):
                j = 2 * i + u
                lanes = pl.ds(pl.multiple_of(j * 128, 128), 128)
                for box in range(2):
                    both = ref[16 * box : 16 * box + 16, lanes].astype(F32)
                    even, odd = swap_lanes(both[:8], both[8:], left)
                    work[2 * j, 8 * box : 8 * box + 8, :] = even
                    work[2 * j + 1, 8 * box : 8 * box + 8, :] = odd
            return carry

        lax.fori_loop(0, N // 4, step, 0)

    def repack(load, ref):
        def step(i, carry):
            for u in range(2):
                j = 2 * i + u
                lanes = pl.ds(pl.multiple_of(j * 128, 128), 128)
                t0, t1 = load(2 * j), load(2 * j + 1)
                for box in range(2):
                    rows = slice(8 * box, 8 * box + 8)
                    lo, hi = swap_lanes(t0[rows], t1[rows], left)
                    ref[16 * box : 16 * box + 16, lanes] = jnp.concatenate([lo, hi], 0).astype(BF16)
            return carry

        lax.fori_loop(0, N // 4, step, 0)

    def pack(m, inner):
        def step(i, carry):
            for u in range(2):
                g = 2 * i + u
                parts = []
                for box in range(2):
                    tiles = [work[4 * g + l, 8 * box : 8 * box + 8, :] for l in range(4)]
                    parts.append(swap_inner(tiles, row4) if inner else swap_outer(tiles, top, left))
                for b in range(4):
                    moves_out[m, 4 * g + b] = jnp.concatenate([parts[0][b], parts[1][b]], 0).astype(BF16)
            return carry

        lax.fori_loop(0, PARTS // 2, step, 0)

    def split(tile):
        return (tile[:8], tile[8:])

    def put(n, v):
        work[n, 0:8, :] = v[0]
        work[n, 8:16, :] = v[1]

    def twiddle(v, row, forward):
        c, s = tw_cos[row], tw_sin[row]
        if forward:
            return (v[0] * c + v[1] * s, v[1] * c - v[0] * s)
        return (v[0] * c - v[1] * s, v[1] * c + v[0] * s)

    def transform_in(load):
        def step(i, carry):
            js = (2 * i, 2 * i + 1)
            loaded = [[split(load(8 * m + j)) for m in range(8)] for j in js]
            for j, xs in zip(js, loaded):
                out = fft8(xs, True)
                put(j, out[0])
                for k1 in range(1, 8):
                    put(8 * k1 + j, twiddle(out[k1], k1 * j, True))
            return carry

        lax.fori_loop(0, 4, step, 0)

    def mix_spectrum(hats, hat, axis, push):
        def step(i, carry):
            k1s = (2 * i, 2 * i + 1)
            spectra = [fft8([split(work[8 * k1 + j]) for j in range(8)], True) for k1 in k1s]
            mixed = []
            for k1, out in zip(k1s, spectra):
                row = []
                for k2 in range(8):
                    k = k1 + 8 * k2
                    conj = k2 >= 4
                    re, im = out[k2]
                    im = -im if conj else im
                    weights = mix[axis, N - k if conj else k]
                    upright = jnp.concatenate([re, im], 0).astype(BF16)
                    if push:
                        turned = jnp.concatenate([im, -re], 0).astype(BF16)
                        v = jnp.concatenate([upright, turned], 1)
                        hats[hat, k] = v
                        y = lax.dot_general(v, weights, (((1,), (1,)), ((), ())), preferred_element_type=F32)
                        re, im = y[:8], y[8:]
                    else:
                        hats[hat, k] = upright
                        y = jnp.dot(upright, weights, preferred_element_type=F32)
                        re, im = y[:8, :128] - y[8:, 128:], y[8:, :128] + y[:8, 128:]
                    row.append((re, -im if conj else im))
                mixed.append(row)
            for k1, row in zip(k1s, mixed):
                back = fft8(row, False)
                for j in range(8):
                    put(8 * k1 + j, twiddle(back[j], k1 * j, False))
            return carry

        lax.fori_loop(0, 4, step, 0)

    def transform_out():
        def step(i, carry):
            js = (2 * i, 2 * i + 1)
            loaded = [[split(work[8 * k1 + j]) for k1 in range(8)] for j in js]
            for j, xs in zip(js, loaded):
                out = fft8(xs, False)
                for m in range(8):
                    put(8 * m + j, out[m])
            return carry

        lax.fori_loop(0, 4, step, 0)

    def arrived(m):
        return lambda n: moves_in[m, n].astype(F32)

    def stage(load, hats, hat, axis, push):
        transform_in(load)
        mix_spectrum(hats, hat, axis, push)
        transform_out()

    def cs_transform(emit):
        def step(k, carry):
            sums = [None] * 4

            def gather(which, term):
                sums[which] = term if sums[which] is None else sums[which] + term

            for t in range(33):
                f = fold[t]
                if t % 2 == 0:
                    gather(t % 4 // 2, f * tw_both[lax.rem(k * t, N)])
                else:
                    gather(2, f * tw_both[lax.rem(k * t, N)])
                    gather(3, f * tw_both[lax.rem((16 - k) * t, N)])
            near = sums[0] + sums[1]
            far = (sums[0] - sums[1]) * sgn
            emit(k, near + sums[2])
            emit(32 - k, (near - sums[2]) * sgn)
            emit(16 - k, far + sums[3])
            emit(16 + k, (far - sums[3]) * sgn)
            return carry

        lax.fori_loop(0, 9, step, 0)

    def make_mix(axis):
        row = lax.broadcasted_iota(jnp.int32, (C, C), 0)
        col = lax.broadcasted_iota(jnp.int32, (C, C), 1)

        def step(i, carry):
            for u in range(3):
                t = 3 * i + u
                later = lax.rem(N - t, N)
                ta = jnp.where(col <= row, taps_v[axis, t].astype(F32), 0.0)
                tb = jnp.where(col <= row, taps_v[axis, later].astype(F32), 0.0)
                once = jnp.logical_or(t == 0, t == 32)
                both = jnp.where(once, ta, ta + tb)
                fold[t] = jnp.concatenate([both, ta - tb], 1).reshape(8, 8, 128)
            return carry

        lax.fori_loop(0, 11, step, 0)

        def emit(k, a):
            a = a * (1.0 / N)
            flipped = swap_halves(a)
            zero = jnp.zeros_like(a)
            rows = jnp.concatenate(
                [
                    jnp.concatenate([jnp.where(left, a, zero), jnp.where(left, flipped, zero)], 2),
                    jnp.concatenate([jnp.where(left, zero, flipped), jnp.where(left, zero, a)], 2),
                ],
                0,
            )
            mix[axis, k] = rows.reshape(128, 256).astype(BF16)

        cs_transform(emit)

    def make_diag():
        row = lax.broadcasted_iota(jnp.int32, (C, C), 0)
        col = lax.broadcasted_iota(jnp.int32, (C, C), 1)
        for axis in range(3):

            def step(i, carry):
                for u in range(4):
                    t = 4 * i + u
                    ta = jnp.where(row == col, taps_v[axis, t].astype(F32), 0.0)
                    diag[axis, pl.ds(t, 1), :] = jnp.sum(ta, 0, keepdims=True)
                return carry

            lax.fori_loop(0, N // 4, step, 0)

    def make_logs():
        highest = lax.Precision.HIGHEST

        def dot(a, b):
            return jnp.dot(a, b, precision=highest, preferred_element_type=F32)

        turns = lax.broadcasted_iota(jnp.int32, (N, N), 0) * lax.broadcasted_iota(jnp.int32, (N, N), 1) % N
        angle = turns.astype(F32) * (2.0 * math.pi / N)
        cos_t, sin_t = jnp.cos(angle), jnp.sin(angle)
        for axis in range(3):
            d = diag[axis]
            real_z, imag_z = dot(cos_t, d), -dot(sin_t, d)
            modulus = real_z * real_z + imag_z * imag_z
            logs[axis] = (dot(cos_t, real_z / modulus) - dot(sin_t, imag_z / modulus)) * (1.0 / math.sqrt(N))

    def grad_terms(axis, cot_hat, field_hat):
        contract = (((0,), (0,)), ((), ()))

        def fill(ps):
            for p, v, u in ps:
                g = lax.dot_general(v, u, contract, preferred_element_type=F32).reshape(2, 8, 8, 256)
                upper_a, upper_b = g[0, :, :, :128], g[0, :, :, 128:]
                lower_a, lower_b = g[1, :, :, :128], g[1, :, :, 128:]
                fold[p] = jnp.where(left, upper_a, lower_b) + swap_halves(jnp.where(left, upper_b, lower_a))

        def pair(p):
            return (
                p,
                jnp.concatenate([cot_hats[cot_hat, p], cot_hats[cot_hat, N - p]], 0),
                jnp.concatenate([field_hats[field_hat, p], field_hats[field_hat, N - p]], 0),
            )

        fill([(p, cot_hats[cot_hat, p], field_hats[field_hat, p]) for p in (0, 32)] + [pair(31)])

        def step(i, carry):
            fill([pair(1 + 3 * i + u) for u in range(3)])
            return carry

        lax.fori_loop(0, 10, step, 0)
        scale = 1.0 / (float(N) ** 2 * math.sqrt(N))

        def emit(t, h):
            h = h * scale
            flipped = swap_halves(h)
            terms[t] = h + flipped
            terms[lax.rem(N - t, N)] = (h - flipped) * sgn

        cs_transform(emit)

        def spread(g, carry):
            for q in range(8):
                part = [jnp.where(left, terms[8 * g + 2 * i, q], terms[8 * g + 2 * i + 1, q]) for i in range(4)]
                a0, b0 = swap_pair(part[0], part[1], top)
                a1, b1 = swap_pair(part[2], part[3], top)
                grad_out[axis, 2 * q, g] = jnp.concatenate([a0, a1], 0).astype(BF16)
                grad_out[axis, 2 * q + 1, g] = jnp.concatenate([b0, b1], 0).astype(BF16)
            return carry

        lax.fori_loop(0, 8, spread, 0)
        start_move("py", *grad_ends(axis))

    def grad_ends(axis):
        return (
            lambda j: grad_out.at[axis, j],
            lambda j: grad_in.at[axis, j],
            gsend_sems.at[axis],
            grecv_sems.at[axis],
        )

    last_ends = (lambda j: last_out.at[j], lambda j: last_in.at[j], lsend_sems, lrecv_sems)

    unpack(cot_ref)
    pack(0, True)
    make_tables()
    pl.semaphore_wait(barrier, jnp.where(same, 3 * PARTS - 3, 3 * PARTS - 2))
    send(0)
    taps_copy.wait()
    make_mix(2)
    unpack(field_ref)
    stage(lambda n: work[n], field_hats, 0, 2, True)
    pack(3, True)
    send(3)

    make_mix(0)
    receive(0)
    stage(arrived(0), cot_hats, 0, 0, False)
    pack(1, False)
    send(1)

    make_mix(1)
    receive(3)
    stage(arrived(3), field_hats, 1, 1, True)
    pack(4, False)
    send(4)

    make_diag()
    forward()
    receive(1)
    stage(arrived(1), cot_hats, 1, 1, False)
    pack(2, True)
    send(2)
    grad_terms(1, 1, 1)

    receive(5)
    stage(arrived(5), field_hats, 2, 0, True)
    pack(6, True)
    send(6)
    receive(2)
    transform_in(arrived(2))
    mix_spectrum(cot_hats, 2, 2, False)
    grad_terms(2, 2, 0)
    grad_terms(0, 0, 2)
    transform_out()
    repack(lambda n: work[n], gfield_ref)
    make_logs()
    receive(6)
    repack(arrived(6), mapped_ref)

    for axis in (1, 2, 0):
        start, end, ssem, rsem = grad_ends(axis)
        wait_in("py", end, ssem, rsem)

    def add_up(g, carry):
        sums = []
        for axis in range(3):
            total = grad_in[axis, 0, g].astype(F32)
            for s in range(1, PARTS):
                total = total + grad_in[axis, s, g].astype(F32)
            sums.append(total)
        for h in range(2):
            rows = slice(8 * h, 8 * h + 8)
            parts = [s[rows] for s in sums] + [jnp.zeros((8, 128), F32)]
            last_out[2 * g + h] = jnp.concatenate(parts, 0).astype(BF16)
        return carry

    lax.fori_loop(0, 8, add_up, 0)
    start_move("px", *last_ends)
    for m in range(7):
        wait_out(KINDS[m], leaving(m), send_sems.at[m], recv_sems.at[m])
    for axis in range(3):
        start, end, ssem, rsem = grad_ends(axis)
        wait_out("py", start, ssem, rsem)
    wait_in("px", last_ends[1], lsend_sems, lrecv_sems)
    total = last_in[0].astype(F32)
    for s in range(1, PARTS):
        total = total + last_in[s].astype(F32)
    row = lax.broadcasted_iota(jnp.int32, (4, C), 0) + 4 * py
    col = lax.broadcasted_iota(jnp.int32, (4, C), 1)
    for axis in range(3):
        for t in range(4):
            rows = slice(8 * axis + 4 * (t // 2), 8 * axis + 4 * (t // 2) + 4)
            own = total[rows, 64 * (t % 2) : 64 * (t % 2) + 64]
            log_row = logs[axis, pl.ds(4 * px + t, 1), :]
            own = own - jnp.where(row == col, log_row, 0.0)
            gtaps_ref[axis, t] = jnp.where(col <= row, own, 0.0)
    wait_out("px", last_ends[0], lsend_sems, lrecv_sems)


def per_device(field, cotangent, taps):
    rows = field.reshape(32, N * C)
    cot_rows = cotangent.transpose(0, 2, 1, 3).reshape(32, N * C)
    vmem = pl.BlockSpec(memory_space=pltpu.VMEM)
    dma = pltpu.SemaphoreType.DMA
    mapped, gfield, gtaps = pl.pallas_call(
        layer_kernel,
        out_shape=(
            jax.ShapeDtypeStruct((32, N * C), BF16),
            jax.ShapeDtypeStruct((32, N * C), BF16),
            jax.ShapeDtypeStruct((3, 4, 4, C), F32),
        ),
        in_specs=[vmem, vmem, pl.BlockSpec(memory_space=pl.ANY)],
        out_specs=(vmem, vmem, vmem),
        scratch_shapes=[
            pltpu.VMEM((3, N, C, C), BF16),
            pltpu.VMEM((N, 8, 128), F32),
            pltpu.VMEM((N, 8, 128), F32),
            pltpu.VMEM((N, 8, 128), F32),
            pltpu.VMEM((33, 8, 8, 128), F32),
            pltpu.VMEM((3, 33, 128, 256), BF16),
            pltpu.VMEM((N, 16, 128), F32),
            pltpu.VMEM((3, N, 16, 128), BF16),
            pltpu.VMEM((3, N, 16, 256), BF16),
            pltpu.VMEM((7, N, 16, 128), BF16),
            pltpu.VMEM((7, N, 16, 128), BF16),
            pltpu.VMEM((N, 8, 8, 128), F32),
            pltpu.VMEM((3, PARTS, 8, 16, 128), BF16),
            pltpu.VMEM((3, PARTS, 8, 16, 128), BF16),
            pltpu.VMEM((PARTS, 32, 128), BF16),
            pltpu.VMEM((PARTS, 32, 128), BF16),
            pltpu.VMEM((3, N, C), F32),
            pltpu.VMEM((3, N, C), F32),
            dma(()),
            dma((7, PARTS)),
            dma((7, PARTS)),
            dma((3, PARTS)),
            dma((3, PARTS)),
            dma((PARTS,)),
            dma((PARTS,)),
        ],
        compiler_params=pltpu.CompilerParams(
            collective_id=0, has_side_effects=True, vmem_limit_bytes=60 * 1024 * 1024
        ),
        name="flow_layer",
    )(rows, cot_rows, taps)
    mapped = mapped.reshape(2, 4, 4, N * C).transpose(0, 2, 1, 3)
    return (mapped, gfield.reshape(2, 4, 4, N * C), gtaps)


def solution(mesh):
    return jax.shard_map(
        per_device,
        mesh=mesh,
        in_specs=(P(None, "px", "py", None), P(None, "px", "py", None), P()),
        out_specs=(P(None, "px", "py", None), P(None, "px", "py", None), P(None, "px", "py", None)),
        check_vma=False,
    )
```

time: 145 us -> 89.5 us (0.62)
  Pallas kernels: 133 us -> 79.3 us
  local copies, waits for them, and re-layouts: 10.3 us -> 8.7 us
    pallas_call x1, Pallas kernels: 133 us -> 79.3 us  [per_device(): pl.pallas_call(layer_kernel, out_shape=(jax.ShapeDtypeStruct((32, N * C),...]
    unnamed x13 -> x1, local copies, waits for them, and re-layouts: 6.28 us -> 1.35 us
where the time goes in v2:
time: 89.5 us; the launch traced here: 88.6 us
  Pallas kernels  79.3 us (89%)
  local copies, waits for them, and re-layouts  8.7 us (10%)
    pallas_call x1, Pallas kernels, per_device(): pl.pallas_call(layer_kernel, out_shape=(jax.ShapeDtypeStruct((32, N * C),...  79.3 us
    reshape x2, local copies, waits for them, and re-layouts, per_device(): mapped = mapped.reshape(2, 4, 4, N * C).transpose(0, 2, 1, 3)  1.96 us

profile of v2, /device:TPU:1, one launch (start us, length us, event | category | flops | bytes accessed | tf_op | source)
XLA Modules:
  0.0 88.6 jit_solution(16635794052915638060)
XLA Ops:
  0.6 1.7 %reshape.18.field_ref = bf16[32,4096]{1,0:T(8,128)(2,1)} reshape(bf16[2,4,4,4096]{3,2,1,0:T(4,128)(2,1)} %param.3) | data formatting | bytes 524288 | tf_op jit(solution)/shard_map/reshape | solution.py:610
  2.3 1.2 %copy.6 = bf16[2,4,4,4096]{3,2,1,0:T(4,128)(2,1)S(1)} copy(bf16[2,4,4,4096]{3,1,2,0:T(4,128)(2,1)} %bitcast.4) | data formatting | bytes 524288 | tf_op jit(solution)/shard_map/transpose | solution.py:611
  3.5 0.8 reshape.19.cot_ref
  4.3 79.3 %flow_layer.1 = (bf16[32,4096]{1,0:T(8,128)(2,1)}, bf16[32,4096]{1,0:T(8,128)(2,1)}, f32[3,4,4,64]{3,2,1,0:T(4,128)}) custom-call(bf16[32,4096]{1,0:T(8,128)(2,1)} %reshape.18.field_ref, bf16[32,4096]{1,0:T(8,128)(2,1)} %reshape.19.cot_ref, bf16[3,64,64,64]{3,2,1,0:T(8,128)(2,1)} %taps_ref.1), custom_call_target="tpu_custom_call" | custom-call | tf_op jit(solution)/shard_map/flow_layer/pallas_call | solution.py:614
  83.5 1.1 %reshape.20 = bf16[2,4,4,4096]{3,2,1,0:T(4,128)(2,1)S(1)} reshape(bf16[32,4096]{1,0:T(8,128)(2,1)} %get-tuple-element.6) | data formatting | bytes 524288 | tf_op jit(solution)/shard_map/reshape | solution.py:655
  84.6 0.9 %copy.9 = bf16[2,4,4,4096]{3,1,2,0:T(4,128)(2,1)} copy(bf16[2,4,4,4096]{3,2,1,0:T(4,128)(2,1)S(1)} %reshape.20) | data formatting | bytes 524288 | tf_op jit(solution)/shard_map/reshape | solution.py:655
  85.5 1.8 %reshape.21 = bf16[2,4,4,4096]{3,2,1,0:T(4,128)(2,1)} reshape(bf16[32,4096]{1,0:T(8,128)(2,1)} %get-tuple-element.7) | data formatting | bytes 524288 | tf_op jit(solution)/shard_map/reshape | solution.py:656
  87.3 1.3 %copy.11 = f32[3,4,4,64]{3,2,1,0:T(4,128)} copy(f32[3,4,4,64]{3,2,1,0:T(4,128)} %get-tuple-element.14) | data formatting | bytes 24576

commit v3 on v2

--- a/solution.py
+++ b/solution.py
@@ -10,6 +10,8 @@
 N = 64
 C = 64
 PARTS = 16
+PAD = 40
+STEP = 72
 MESH = pl.DeviceIdType.MESH
 F32 = jnp.float32
 BF16 = jnp.bfloat16
@@ -94,25 +96,32 @@
     mapped_ref,
     gfield_ref,
     gtaps_ref,
+    field_v,
+    cot_v,
+    mapped_v,
+    gfield_v,
     taps_v,
     tw_cos,
     tw_sin,
-    tw_both,
-    fold,
+    mix_table,
+    grad_table,
+    wide,
+    spec,
     mix,
     work,
     cot_hats,
     field_hats,
     moves_out,
     moves_in,
-    terms,
     grad_out,
     grad_in,
+    last_rows,
     last_out,
     last_in,
+    last_sum,
     diag,
     logs,
-    taps_sem,
+    io_sems,
     send_sems,
     recv_sems,
     gsend_sems,
@@ -125,6 +134,15 @@
     same = px == py
     differ = jnp.logical_not(same)
 
+    cot_copy = pltpu.make_async_copy(cot_ref, cot_v, io_sems.at[0])
+    taps_copy = pltpu.make_async_copy(taps_ref, taps_v, io_sems.at[1])
+    field_copy = pltpu.make_async_copy(field_ref, field_v, io_sems.at[2])
+    gfield_copy = pltpu.make_async_copy(gfield_v, gfield_ref, io_sems.at[3])
+    mapped_copy = pltpu.make_async_copy(mapped_v, mapped_ref, io_sems.at[4])
+    cot_copy.start()
+    taps_copy.start()
+    field_copy.start()
+
     barrier = pltpu.get_barrier_semaphore()
 
     def greet(i, carry):
@@ -144,11 +162,9 @@
 
     lax.fori_loop(0, PARTS, greet, 0)
 
-    taps_copy = pltpu.make_async_copy(taps_ref, taps_v, taps_sem)
-    taps_copy.start()
-
     left = lax.broadcasted_iota(jnp.int32, (8, 128), 1) < 64
-    sgn = jnp.where(left, 1.0, -1.0).astype(F32)
+    left_n = lax.broadcasted_iota(jnp.int32, (N, 128), 1) < 64
+    left_p = lax.broadcasted_iota(jnp.int32, (PAD, 128), 1) < 64
     row8 = lax.broadcasted_iota(jnp.int32, (8, 128), 0)
     row4 = row8 % 4
     top = row8 < 4
@@ -161,7 +177,23 @@
             s = jnp.broadcast_to(sin[r : r + 1, :], (8, 128))
             tw_cos[r] = c
             tw_sin[r] = s
-            tw_both[r] = jnp.where(left, c, s)
+
+        def waves(turns):
+            angle = (turns & (N - 1)).astype(F32) * (2.0 * math.pi / N)
+            return jnp.cos(angle), jnp.sin(angle)
+
+        row = lax.broadcasted_iota(jnp.int32, (2 * PAD, N), 0)
+        t = lax.broadcasted_iota(jnp.int32, (2 * PAD, N), 1)
+        cos, sin = waves(jnp.where(row < PAD, row, row - PAD) * t)
+        mix_table[...] = (jnp.where(row < PAD, cos, sin) * (1.0 / N)).astype(BF16)
+        r = lax.broadcasted_iota(jnp.int32, (64, 2 * PAD), 0)
+        col = lax.broadcasted_iota(jnp.int32, (64, 2 * PAD), 1)
+        p = jnp.where(col < PAD, col, col - PAD)
+        t = 4 * (r & 15) + 2 * ((r & 31) >> 4) + (r >> 5)
+        cos, sin = waves(p * t)
+        scale = 1.0 / (float(N) ** 2 * math.sqrt(N))
+        value = jnp.where((r < 32) == (col < PAD), cos, sin) * scale
+        grad_table[...] = jnp.where(p <= 32, value, 0.0).astype(BF16)
 
     def move_route(kind, j):
         if kind == "py":
@@ -256,38 +288,58 @@
 
         lax.fori_loop(0, PARTS, step, 0)
 
-    def unpack(ref):
-        def step(i, carry):
-            for u in range(2):
-                j = 2 * i + u
+    def flip_cells(v):
+        a0, b0 = row8 // 4, row8 % 2
+        v = jnp.where(a0 == b0, v, jnp.where(a0 < b0, pltpu.roll(v, 5, 0), pltpu.roll(v, 3, 0)))
+        lane_bit = jnp.where(left, 0, 1)
+        b1 = row8 // 2 % 2
+        turned = swap_halves(v)
+        return jnp.where(
+            lane_bit == b1, v, jnp.where(b1 < lane_bit, pltpu.roll(turned, 6, 0), pltpu.roll(turned, 2, 0))
+        )
+
+    def unpack(ref, flip):
+        def step(i, carry):
+            for u in range(8):
+                j = 8 * i + u
                 lanes = pl.ds(pl.multiple_of(j * 128, 128), 128)
                 for box in range(2):
-                    both = ref[16 * box : 16 * box + 16, lanes].astype(F32)
-                    even, odd = swap_lanes(both[:8], both[8:], left)
+                    rows = [ref[box, x, :, lanes].astype(F32) for x in range(4)]
+                    even, odd = swap_lanes(
+                        jnp.concatenate(rows[:2], 0), jnp.concatenate(rows[2:], 0), left
+                    )
+                    if flip:
+                        even, odd = flip_cells(even), flip_cells(odd)
                     work[2 * j, 8 * box : 8 * box + 8, :] = even
                     work[2 * j + 1, 8 * box : 8 * box + 8, :] = odd
             return carry
 
-        lax.fori_loop(0, N // 4, step, 0)
-
-    def repack(load, ref):
-        def step(i, carry):
-            for u in range(2):
-                j = 2 * i + u
+        lax.fori_loop(0, N // 16, step, 0)
+
+    def repack(load, ref, flip):
+        def step(i, carry):
+            for u in range(8):
+                j = 8 * i + u
                 lanes = pl.ds(pl.multiple_of(j * 128, 128), 128)
                 t0, t1 = load(2 * j), load(2 * j + 1)
                 for box in range(2):
                     rows = slice(8 * box, 8 * box + 8)
-                    lo, hi = swap_lanes(t0[rows], t1[rows], left)
-                    ref[16 * box : 16 * box + 16, lanes] = jnp.concatenate([lo, hi], 0).astype(BF16)
-            return carry
-
-        lax.fori_loop(0, N // 4, step, 0)
+                    v0, v1 = t0[rows], t1[rows]
+                    if flip:
+                        v0, v1 = flip_cells(v0), flip_cells(v1)
+                    lo, hi = swap_lanes(v0, v1, left)
+                    ref[box, 0, :, lanes] = lo[:4].astype(BF16)
+                    ref[box, 1, :, lanes] = lo[4:].astype(BF16)
+                    ref[box, 2, :, lanes] = hi[:4].astype(BF16)
+                    ref[box, 3, :, lanes] = hi[4:].astype(BF16)
+            return carry
+
+        lax.fori_loop(0, N // 16, step, 0)
 
     def pack(m, inner):
         def step(i, carry):
-            for u in range(2):
-                g = 2 * i + u
+            for u in range(4):
+                g = 4 * i + u
                 parts = []
                 for box in range(2):
                     tiles = [work[4 * g + l, 8 * box : 8 * box + 8, :] for l in range(4)]
@@ -296,7 +348,7 @@
                     moves_out[m, 4 * g + b] = jnp.concatenate([parts[0][b], parts[1][b]], 0).astype(BF16)
             return carry
 
-        lax.fori_loop(0, PARTS // 2, step, 0)
+        lax.fori_loop(0, PARTS // 4, step, 0)
 
     def split(tile):
         return (tile[:8], tile[8:])
@@ -378,61 +430,47 @@
         mix_spectrum(hats, hat, axis, push)
         transform_out()
 
-    def cs_transform(emit):
-        def step(k, carry):
-            sums = [None] * 4
-
-            def gather(which, term):
-                sums[which] = term if sums[which] is None else sums[which] + term
-
-            for t in range(33):
-                f = fold[t]
-                if t % 2 == 0:
-                    gather(t % 4 // 2, f * tw_both[lax.rem(k * t, N)])
-                else:
-                    gather(2, f * tw_both[lax.rem(k * t, N)])
-                    gather(3, f * tw_both[lax.rem((16 - k) * t, N)])
-            near = sums[0] + sums[1]
-            far = (sums[0] - sums[1]) * sgn
-            emit(k, near + sums[2])
-            emit(32 - k, (near - sums[2]) * sgn)
-            emit(16 - k, far + sums[3])
-            emit(16 + k, (far - sums[3]) * sgn)
-            return carry
-
-        lax.fori_loop(0, 9, step, 0)
-
     def make_mix(axis):
         row = lax.broadcasted_iota(jnp.int32, (C, C), 0)
         col = lax.broadcasted_iota(jnp.int32, (C, C), 1)
 
-        def step(i, carry):
-            for u in range(3):
-                t = 3 * i + u
-                later = lax.rem(N - t, N)
+        def widen(i, carry):
+            for u in range(16):
+                t = 16 * i + u
                 ta = jnp.where(col <= row, taps_v[axis, t].astype(F32), 0.0)
-                tb = jnp.where(col <= row, taps_v[axis, later].astype(F32), 0.0)
-                once = jnp.logical_or(t == 0, t == 32)
-                both = jnp.where(once, ta, ta + tb)
-                fold[t] = jnp.concatenate([both, ta - tb], 1).reshape(8, 8, 128)
-            return carry
-
-        lax.fori_loop(0, 11, step, 0)
-
-        def emit(k, a):
-            a = a * (1.0 / N)
-            flipped = swap_halves(a)
-            zero = jnp.zeros_like(a)
-            rows = jnp.concatenate(
-                [
-                    jnp.concatenate([jnp.where(left, a, zero), jnp.where(left, flipped, zero)], 2),
-                    jnp.concatenate([jnp.where(left, zero, flipped), jnp.where(left, zero, a)], 2),
-                ],
-                0,
-            )
-            mix[axis, k] = rows.reshape(128, 256).astype(BF16)
-
-        cs_transform(emit)
+                wide[pl.ds(pl.multiple_of(t * STEP, 8), C), :] = jnp.concatenate([ta, ta], 1)
+            return carry
+
+        lax.fori_loop(0, N // 16, widen, 0)
+
+        def transform(i, carry):
+            for u in range(8):
+                co = 16 * i + 2 * u
+                x = [wide[pl.ds(co + v, N, stride=STEP), :] for v in range(2)]
+                both = jnp.concatenate(x, 1).astype(BF16)
+                out = jnp.dot(mix_table[...], both, preferred_element_type=F32)
+                for v in range(2):
+                    lanes = slice(128 * v, 128 * v + 128)
+                    spec[pl.ds(co + v, PAD, stride=STEP), :] = jnp.where(left_p, out[:PAD, lanes], out[PAD:, lanes])
+            return carry
+
+        lax.fori_loop(0, C // 16, transform, 0)
+
+        def place(i, carry):
+            for u in range(11):
+                k = 11 * i + u
+                a = spec[pl.ds(pl.multiple_of(k * STEP, 8), C), :]
+                flipped = swap_halves(a)
+                mix[axis, k] = jnp.concatenate(
+                    [
+                        jnp.concatenate([jnp.where(left_n, a, 0.0), jnp.where(left_n, flipped, 0.0)], 1),
+                        jnp.concatenate([jnp.where(left_n, 0.0, flipped), jnp.where(left_n, 0.0, a)], 1),
+                    ],
+                    0,
+                ).astype(BF16)
+            return carry
+
+        lax.fori_loop(0, 3, place, 0)
 
     def make_diag():
         row = lax.broadcasted_iota(jnp.int32, (C, C), 0)
@@ -440,13 +478,13 @@
         for axis in range(3):
 
             def step(i, carry):
-                for u in range(4):
-                    t = 4 * i + u
+                for u in range(16):
+                    t = 16 * i + u
                     ta = jnp.where(row == col, taps_v[axis, t].astype(F32), 0.0)
                     diag[axis, pl.ds(t, 1), :] = jnp.sum(ta, 0, keepdims=True)
                 return carry
 
-            lax.fori_loop(0, N // 4, step, 0)
+            lax.fori_loop(0, N // 16, step, 0)
 
     def make_logs():
         highest = lax.Precision.HIGHEST
@@ -468,45 +506,54 @@
 
         def fill(ps):
             for p, v, u in ps:
-                g = lax.dot_general(v, u, contract, preferred_element_type=F32).reshape(2, 8, 8, 256)
-                upper_a, upper_b = g[0, :, :, :128], g[0, :, :, 128:]
-                lower_a, lower_b = g[1, :, :, :128], g[1, :, :, 128:]
-                fold[p] = jnp.where(left, upper_a, lower_b) + swap_halves(jnp.where(left, upper_b, lower_a))
-
-        def pair(p):
+                g = lax.dot_general(v, u, contract, preferred_element_type=F32)
+                spec[pl.ds(pl.multiple_of(p * STEP, 8), C), :] = g
+
+        def cot_rows(k):
+            v = cot_hats[cot_hat, k]
+            return [v[:, :64], v[:, 64:]]
+
+        def field_rows(k):
+            u = field_hats[field_hat, k]
+            return [
+                jnp.concatenate([u[:, :64], u[:, 128:192]], 1),
+                jnp.concatenate([u[:, 64:128], u[:, 192:]], 1),
+            ]
+
+        def operands(p, ks):
             return (
                 p,
-                jnp.concatenate([cot_hats[cot_hat, p], cot_hats[cot_hat, N - p]], 0),
-                jnp.concatenate([field_hats[field_hat, p], field_hats[field_hat, N - p]], 0),
+                jnp.concatenate(sum([cot_rows(k) for k in ks], []), 0),
+                jnp.concatenate(sum([field_rows(k) for k in ks], []), 0),
             )
 
-        fill([(p, cot_hats[cot_hat, p], field_hats[field_hat, p]) for p in (0, 32)] + [pair(31)])
-
-        def step(i, carry):
-            fill([pair(1 + 3 * i + u) for u in range(3)])
-            return carry
-
-        lax.fori_loop(0, 10, step, 0)
-        scale = 1.0 / (float(N) ** 2 * math.sqrt(N))
-
-        def emit(t, h):
-            h = h * scale
-            flipped = swap_halves(h)
-            terms[t] = h + flipped
-            terms[lax.rem(N - t, N)] = (h - flipped) * sgn
-
-        cs_transform(emit)
-
-        def spread(g, carry):
-            for q in range(8):
-                part = [jnp.where(left, terms[8 * g + 2 * i, q], terms[8 * g + 2 * i + 1, q]) for i in range(4)]
-                a0, b0 = swap_pair(part[0], part[1], top)
-                a1, b1 = swap_pair(part[2], part[3], top)
-                grad_out[axis, 2 * q, g] = jnp.concatenate([a0, a1], 0).astype(BF16)
-                grad_out[axis, 2 * q + 1, g] = jnp.concatenate([b0, b1], 0).astype(BF16)
-            return carry
-
-        lax.fori_loop(0, 8, spread, 0)
+        def pair(p):
+            return operands(p, (p, N - p))
+
+        fill([operands(0, (0,)), operands(32, (32,)), pair(31)])
+
+        def step(i, carry):
+            fill([pair(1 + 10 * i + u) for u in range(10)])
+            return carry
+
+        lax.fori_loop(0, 3, step, 0)
+
+        def spread(i, carry):
+            for u in range(8):
+                part = 4 * i + u // 2
+                co = 4 * part + 2 * (u % 2)
+                x = [spec[pl.ds(co + v, PAD, stride=STEP), :] for v in range(2)]
+                both = jnp.concatenate([jnp.concatenate([v, swap_halves(v)], 0) for v in x], 1)
+                out = jnp.dot(grad_table[...], both.astype(BF16), preferred_element_type=F32)
+                for v in range(2):
+                    lanes = slice(128 * v, 128 * v + 128)
+                    at = 32 * (2 * (u % 2) + v)
+                    grad_out[axis, part, at : at + 32, :] = jnp.where(
+                        left_p[:32], out[:32, lanes], out[32:, lanes]
+                    ).astype(BF16)
+            return carry
+
+        lax.fori_loop(0, PARTS // 4, spread, 0)
         start_move("py", *grad_ends(axis))
 
     def grad_ends(axis):
@@ -519,14 +566,16 @@
 
     last_ends = (lambda j: last_out.at[j], lambda j: last_in.at[j], lsend_sems, lrecv_sems)
 
-    unpack(cot_ref)
+    cot_copy.wait()
+    unpack(cot_v, True)
     pack(0, True)
-    make_tables()
     pl.semaphore_wait(barrier, jnp.where(same, 3 * PARTS - 3, 3 * PARTS - 2))
     send(0)
+    make_tables()
     taps_copy.wait()
     make_mix(2)
-    unpack(field_ref)
+    field_copy.wait()
+    unpack(field_v, False)
     stage(lambda n: work[n], field_hats, 0, 2, True)
     pack(3, True)
     send(3)
@@ -549,41 +598,47 @@
     stage(arrived(1), cot_hats, 1, 1, False)
     pack(2, True)
     send(2)
+
     grad_terms(1, 1, 1)
-
+    receive(2)
+    transform_in(arrived(2))
+    mix_spectrum(cot_hats, 2, 2, False)
+    grad_terms(2, 2, 0)
+    transform_out()
+    repack(lambda n: work[n], gfield_v, False)
+    gfield_copy.start()
     receive(5)
     stage(arrived(5), field_hats, 2, 0, True)
     pack(6, True)
     send(6)
-    receive(2)
-    transform_in(arrived(2))
-    mix_spectrum(cot_hats, 2, 2, False)
-    grad_terms(2, 2, 0)
+
     grad_terms(0, 0, 2)
-    transform_out()
-    repack(lambda n: work[n], gfield_ref)
+
     make_logs()
     receive(6)
-    repack(arrived(6), mapped_ref)
+    repack(arrived(6), mapped_v, True)
+    mapped_copy.start()
 
     for axis in (1, 2, 0):
         start, end, ssem, rsem = grad_ends(axis)
         wait_in("py", end, ssem, rsem)
 
-    def add_up(g, carry):
-        sums = []
-        for axis in range(3):
-            total = grad_in[axis, 0, g].astype(F32)
+    last_rows[...] = jnp.zeros_like(last_rows)
+    for axis in range(3):
+
+        def add_up(c, carry):
+            rows = pl.ds(pl.multiple_of(32 * c, 32), 32)
+            total = grad_in[axis, 0, rows, :].astype(F32)
             for s in range(1, PARTS):
-                total = total + grad_in[axis, s, g].astype(F32)
-            sums.append(total)
-        for h in range(2):
-            rows = slice(8 * h, 8 * h + 8)
-            parts = [s[rows] for s in sums] + [jnp.zeros((8, 128), F32)]
-            last_out[2 * g + h] = jnp.concatenate(parts, 0).astype(BF16)
-        return carry
-
-    lax.fori_loop(0, 8, add_up, 0)
+                total = total + grad_in[axis, s, rows, :].astype(F32)
+            for h in range(2):
+                last_rows[pl.ds(8 * axis + 2 * c + h, PARTS, stride=32), :] = total[16 * h : 16 * h + 16]
+            return carry
+
+        lax.fori_loop(0, 4, add_up, 0)
+
+    for j in range(PARTS):
+        last_out[j] = last_rows[32 * j : 32 * j + 32, :].astype(BF16)
     start_move("px", *last_ends)
     for m in range(7):
         wait_out(KINDS[m], leaving(m), send_sems.at[m], recv_sems.at[m])
@@ -594,52 +649,75 @@
     total = last_in[0].astype(F32)
     for s in range(1, PARTS):
         total = total + last_in[s].astype(F32)
+    last_sum[...] = total
     row = lax.broadcasted_iota(jnp.int32, (4, C), 0) + 4 * py
     col = lax.broadcasted_iota(jnp.int32, (4, C), 1)
     for axis in range(3):
         for t in range(4):
-            rows = slice(8 * axis + 4 * (t // 2), 8 * axis + 4 * (t // 2) + 4)
-            own = total[rows, 64 * (t % 2) : 64 * (t % 2) + 64]
+            own = last_sum[pl.ds(8 * axis + t // 2, 4, stride=2), :]
+            own = own[:, 64 * (t % 2) : 64 * (t % 2) + 64]
             log_row = logs[axis, pl.ds(4 * px + t, 1), :]
             own = own - jnp.where(row == col, log_row, 0.0)
             gtaps_ref[axis, t] = jnp.where(col <= row, own, 0.0)
     wait_out("px", last_ends[0], lsend_sems, lrecv_sems)
+    gfield_copy.wait()
+    mapped_copy.wait()
+
+
+def hand_over_kernel(mapped_in, gfield_in, gtaps_in, mapped_out, gfield_out, gtaps_out, a, b, c, sems):
+    legs = ((mapped_in, a, mapped_out), (gfield_in, b, gfield_out), (gtaps_in, c, gtaps_out))
+    inward = [pltpu.make_async_copy(src, mid, sems.at[0, i]) for i, (src, mid, _) in enumerate(legs)]
+    outward = [pltpu.make_async_copy(mid, dst, sems.at[1, i]) for i, (_, mid, dst) in enumerate(legs)]
+    for copy in inward:
+        copy.start()
+    for first, second in zip(inward, outward):
+        first.wait()
+        second.start()
+    for copy in outward:
+        copy.wait()
 
 
 def per_device(field, cotangent, taps):
-    rows = field.reshape(32, N * C)
-    cot_rows = cotangent.transpose(0, 2, 1, 3).reshape(32, N * C)
     vmem = pl.BlockSpec(memory_space=pltpu.VMEM)
+    anywhere = pl.BlockSpec(memory_space=pl.ANY)
     dma = pltpu.SemaphoreType.DMA
-    mapped, gfield, gtaps = pl.pallas_call(
+    shapes = (
+        jax.ShapeDtypeStruct((2, 4, 4, N * C), BF16),
+        jax.ShapeDtypeStruct((2, 4, 4, N * C), BF16),
+        jax.ShapeDtypeStruct((3, 4, 4, C), F32),
+    )
+    results = pl.pallas_call(
         layer_kernel,
-        out_shape=(
-            jax.ShapeDtypeStruct((32, N * C), BF16),
-            jax.ShapeDtypeStruct((32, N * C), BF16),
-            jax.ShapeDtypeStruct((3, 4, 4, C), F32),
-        ),
-        in_specs=[vmem, vmem, pl.BlockSpec(memory_space=pl.ANY)],
-        out_specs=(vmem, vmem, vmem),
+        out_shape=shapes,
+        in_specs=[anywhere] * 3,
+        out_specs=(anywhere, anywhere, vmem),
         scratch_shapes=[
+            pltpu.VMEM((2, 4, 4, N * C), BF16),
+            pltpu.VMEM((2, 4, 4, N * C), BF16),
+            pltpu.VMEM((2, 4, 4, N * C), BF16),
+            pltpu.VMEM((2, 4, 4, N * C), BF16),
             pltpu.VMEM((3, N, C, C), BF16),
             pltpu.VMEM((N, 8, 128), F32),
             pltpu.VMEM((N, 8, 128), F32),
-            pltpu.VMEM((N, 8, 128), F32),
-            pltpu.VMEM((33, 8, 8, 128), F32),
+            pltpu.VMEM((2 * PAD, N), BF16),
+            pltpu.VMEM((64, 2 * PAD), BF16),
+            pltpu.VMEM((N * STEP, 128), F32),
+            pltpu.VMEM((PAD * STEP, 128), F32),
             pltpu.VMEM((3, 33, 128, 256), BF16),
             pltpu.VMEM((N, 16, 128), F32),
             pltpu.VMEM((3, N, 16, 128), BF16),
             pltpu.VMEM((3, N, 16, 256), BF16),
             pltpu.VMEM((7, N, 16, 128), BF16),
             pltpu.VMEM((7, N, 16, 128), BF16),
-            pltpu.VMEM((N, 8, 8, 128), F32),
-            pltpu.VMEM((3, PARTS, 8, 16, 128), BF16),
-            pltpu.VMEM((3, PARTS, 8, 16, 128), BF16),
+            pltpu.VMEM((3, PARTS, 128, 128), BF16),
+            pltpu.VMEM((3, PARTS, 128, 128), BF16),
+            pltpu.VMEM((PARTS * 32, 128), F32),
             pltpu.VMEM((PARTS, 32, 128), BF16),
             pltpu.VMEM((PARTS, 32, 128), BF16),
+            pltpu.VMEM((32, 128), F32),
             pltpu.VMEM((3, N, C), F32),
             pltpu.VMEM((3, N, C), F32),
-            dma(()),
+            dma((5,)),
             dma((7, PARTS)),
             dma((7, PARTS)),
             dma((3, PARTS)),
@@ -651,9 +729,16 @@
             collective_id=0, has_side_effects=True, vmem_limit_bytes=60 * 1024 * 1024
         ),
         name="flow_layer",
-    )(rows, cot_rows, taps)
-    mapped = mapped.reshape(2, 4, 4, N * C).transpose(0, 2, 1, 3)
-    return (mapped, gfield.reshape(2, 4, 4, N * C), gtaps)
+    )(field, cotangent, taps)
+    return pl.pallas_call(
+        hand_over_kernel,
+        out_shape=shapes,
+        in_specs=[anywhere] * 3,
+        out_specs=(anywhere,) * 3,
+        scratch_shapes=[pltpu.VMEM(a.shape, a.dtype) for a in shapes] + [dma((2, 3))],
+        compiler_params=pltpu.CompilerParams(vmem_limit_bytes=60 * 1024 * 1024),
+        name="hand_over",
+    )(*results)
 
 
 def solution(mesh):

time: 89.5 us -> 77.8 us (0.87)
  local copies, waits for them, and re-layouts: 8.7 us -> 0 us
  Pallas kernels: 79.3 us -> 77.1 us
    reshape x5 -> x0, local copies, waits for them, and re-layouts: 6.2 us -> none  [the longest x2 1.96 us: per_device(): mapped = mapped.reshape(2, 4, 4, N * C).transpose(0, 2, 1, 3)]
    pallas_call x1 -> x2, Pallas kernels: 79.3 us -> 77.1 us  [the longest x1 75.3 us: per_device(): pl.pallas_call(layer_kernel, out_shape=shapes, in_specs=[anywhere] * 3, o...]
    unnamed x1 -> x0, local copies, waits for them, and re-layouts: 1.35 us -> none
    transpose x1 -> x0, local copies, waits for them, and re-layouts: 1.16 us -> none  [per_device(): cot_rows = cotangent.transpose(0, 2, 1, 3).reshape(32, N * C)]
where the time goes in v3:
time: 77.8 us; the launch traced here: 77.7 us
  Pallas kernels  77.1 us (99%)
    pallas_call x1, Pallas kernels, per_device(): pl.pallas_call(layer_kernel, out_shape=shapes, in_specs=[anywhere] * 3, o...  75.3 us
    pallas_call x1, Pallas kernels, per_device(): pl.pallas_call(hand_over_kernel, out_shape=shapes, in_specs=[anywhere] *...  1.79 us

profile of v3, /device:TPU:1, one launch (start us, length us, event | category | flops | bytes accessed | tf_op | source)
XLA Modules:
  0.0 77.7 jit_solution(7965537856128923966)
XLA Ops:
  0.6 75.3 %flow_layer.1 = (bf16[2,4,4,4096]{3,2,1,0:T(4,128)(2,1)}, bf16[2,4,4,4096]{3,2,1,0:T(4,128)(2,1)}, f32[3,4,4,64]{3,2,1,0:T(4,128)}) custom-call(bf16[2,4,4,4096]{3,2,1,0:T(4,128)(2,1)} %field_ref.1, bf16[2,4,4,4096]{3,2,1,0:T(4,128)(2,1)} %cot_ref.1, bf16[3,64,64,64]{3,2,1,0:T(8,128)(2,1)} %taps_ref.1), custom_call_target="tpu_custom_call" | custom-call | tf_op jit(solution)/shard_map/flow_layer/pallas_call | solution.py:689
  75.9 1.8 %hand_over.1 = (bf16[2,4,4,4096]{3,2,1,0:T(4,128)(2,1)}, bf16[2,4,4,4096]{3,2,1,0:T(4,128)(2,1)}, f32[3,4,4,64]{3,2,1,0:T(4,128)}) custom-call(bf16[2,4,4,4096]{3,2,1,0:T(4,128)(2,1)} %get-tuple-element.6.mapped_in, bf16[2,4,4,4096]{3,2,1,0:T(4,128)(2,1)} %get-tuple-element.7.gfield_in, f32[3,4,4,64]{3,2,1,0:T(4,128)} %get-tuple-element.8.gtaps_in), custom_call_target="tpu_custom_call" | custom-call | tf_op jit(solution)/shard_map/hand_over/pallas_call | solution.py:733

commit v4 on v3

--- a/solution.py
+++ b/solution.py
@@ -108,7 +108,8 @@
     wide,
     spec,
     mix,
-    work,
+    work_a,
+    work_b,
     cot_hats,
     field_hats,
     moves_out,
@@ -132,6 +133,7 @@
     px = lax.axis_index("px")
     py = lax.axis_index("py")
     same = px == py
+    work = work_a
     differ = jnp.logical_not(same)
 
     cot_copy = pltpu.make_async_copy(cot_ref, cot_v, io_sems.at[0])
@@ -601,30 +603,31 @@
 
     grad_terms(1, 1, 1)
     receive(2)
+    work = work_b
     transform_in(arrived(2))
     mix_spectrum(cot_hats, 2, 2, False)
     grad_terms(2, 2, 0)
+    receive(5)
+    work = work_a
+    stage(arrived(5), field_hats, 2, 0, True)
+    pack(6, True)
+    send(6)
+
+    grad_terms(0, 0, 2)
+    work = work_b
     transform_out()
     repack(lambda n: work[n], gfield_v, False)
     gfield_copy.start()
-    receive(5)
-    stage(arrived(5), field_hats, 2, 0, True)
-    pack(6, True)
-    send(6)
-
-    grad_terms(0, 0, 2)
 
     make_logs()
     receive(6)
     repack(arrived(6), mapped_v, True)
     mapped_copy.start()
 
+    last_rows[...] = jnp.zeros_like(last_rows)
     for axis in (1, 2, 0):
         start, end, ssem, rsem = grad_ends(axis)
         wait_in("py", end, ssem, rsem)
-
-    last_rows[...] = jnp.zeros_like(last_rows)
-    for axis in range(3):
 
         def add_up(c, carry):
             rows = pl.ds(pl.multiple_of(32 * c, 32), 32)
@@ -704,6 +707,7 @@
             pltpu.VMEM((N * STEP, 128), F32),
             pltpu.VMEM((PAD * STEP, 128), F32),
             pltpu.VMEM((3, 33, 128, 256), BF16),
+            pltpu.VMEM((N, 16, 128), F32),
             pltpu.VMEM((N, 16, 128), F32),
             pltpu.VMEM((3, N, 16, 128), BF16),
             pltpu.VMEM((3, N, 16, 256), BF16),

time: 77.8 us -> 78.3 us (level)
  no operation moved by 1% of the time
where the time goes in v4:
time: 78.3 us; the launch traced here: 78.2 us
  Pallas kernels  77.6 us (99%)
    pallas_call x1, Pallas kernels, per_device(): pl.pallas_call(layer_kernel, out_shape=shapes, in_specs=[anywhere] * 3, o...  75.8 us
    pallas_call x1, Pallas kernels, per_device(): pl.pallas_call(hand_over_kernel, out_shape=shapes, in_specs=[anywhere] *...  1.79 us

profile of v4, /device:TPU:1, one launch (start us, length us, event | category | flops | bytes accessed | tf_op | source)
XLA Modules:
  0.0 78.2 jit_solution(9253045237118744816)
XLA Ops:
  0.6 75.8 %flow_layer.1 = (bf16[2,4,4,4096]{3,2,1,0:T(4,128)(2,1)}, bf16[2,4,4,4096]{3,2,1,0:T(4,128)(2,1)}, f32[3,4,4,64]{3,2,1,0:T(4,128)}) custom-call(bf16[2,4,4,4096]{3,2,1,0:T(4,128)(2,1)} %field_ref.1, bf16[2,4,4,4096]{3,2,1,0:T(4,128)(2,1)} %cot_ref.1, bf16[3,64,64,64]{3,2,1,0:T(8,128)(2,1)} %taps_ref.1), custom_call_target="tpu_custom_call" | custom-call | tf_op jit(solution)/shard_map/flow_layer/pallas_call | solution.py:692
  76.4 1.8 %hand_over.1 = (bf16[2,4,4,4096]{3,2,1,0:T(4,128)(2,1)}, bf16[2,4,4,4096]{3,2,1,0:T(4,128)(2,1)}, f32[3,4,4,64]{3,2,1,0:T(4,128)}) custom-call(bf16[2,4,4,4096]{3,2,1,0:T(4,128)(2,1)} %get-tuple-element.6.mapped_in, bf16[2,4,4,4096]{3,2,1,0:T(4,128)(2,1)} %get-tuple-element.7.gfield_in, f32[3,4,4,64]{3,2,1,0:T(4,128)} %get-tuple-element.8.gtaps_in), custom_call_target="tpu_custom_call" | custom-call | tf_op jit(solution)/shard_map/hand_over/pallas_call | solution.py:737

commit v5 on v3

--- a/solution.py
+++ b/solution.py
@@ -538,28 +538,51 @@
 
         lax.fori_loop(0, 3, step, 0)
 
-        def spread(i, carry):
+        def spread(i, carry, narrow):
             for u in range(8):
                 part = 4 * i + u // 2
                 co = 4 * part + 2 * (u % 2)
                 x = [spec[pl.ds(co + v, PAD, stride=STEP), :] for v in range(2)]
                 both = jnp.concatenate([jnp.concatenate([v, swap_halves(v)], 0) for v in x], 1)
                 out = jnp.dot(grad_table[...], both.astype(BF16), preferred_element_type=F32)
-                for v in range(2):
-                    lanes = slice(128 * v, 128 * v + 128)
-                    at = 32 * (2 * (u % 2) + v)
-                    grad_out[axis, part, at : at + 32, :] = jnp.where(
-                        left_p[:32], out[:32, lanes], out[32:, lanes]
-                    ).astype(BF16)
-            return carry
-
-        lax.fori_loop(0, PARTS // 4, spread, 0)
-        start_move("py", *grad_ends(axis))
-
-    def grad_ends(axis):
+                a, b = [
+                    jnp.where(left_p[:32], out[:32, 128 * v : 128 * v + 128], out[32:, 128 * v : 128 * v + 128])
+                    for v in range(2)
+                ]
+                if narrow:
+                    at = 32 * (u % 2)
+                    grad_out[axis, part, at : at + 32, :] = jnp.where(low_half, a, pltpu.roll(b, 32, 1)).astype(BF16)
+                else:
+                    at = 64 * (u % 2)
+                    grad_out[axis, part, at : at + 32, :] = a.astype(BF16)
+                    grad_out[axis, part, at + 32 : at + 64, :] = b.astype(BF16)
+            return carry
+
+        low_half = lax.broadcasted_iota(jnp.int32, (32, 128), 1) % 64 < 32
+        lax.fori_loop(0, 2, lambda i, carry: spread(i, carry, True), 0)
+        lax.fori_loop(2, 4, lambda i, carry: spread(i, carry, False), 0)
+
+        def go(i, carry):
+            j = lax.rem(py + 1 + i, PARTS)
+            for size, here in ((64, j < 8), (128, j >= 8)):
+                start, end, ssem, rsem = grad_ends(axis, size)
+
+                @pl.when(jnp.logical_and(here, j == py))
+                def _():
+                    end(py)[...] = start(j)[...]
+
+                @pl.when(jnp.logical_and(here, j != py))
+                def _():
+                    remote(start(j), end(py), ssem.at[j], rsem.at[py], (px, j)).start()
+
+            return carry
+
+        lax.fori_loop(0, PARTS, go, 0)
+
+    def grad_ends(axis, size):
         return (
-            lambda j: grad_out.at[axis, j],
-            lambda j: grad_in.at[axis, j],
+            lambda j: grad_out.at[axis, j, pl.ds(0, size)],
+            lambda j: grad_in.at[axis, j, pl.ds(0, size)],
             gsend_sems.at[axis],
             grecv_sems.at[axis],
         )
@@ -619,23 +642,36 @@
     repack(arrived(6), mapped_v, True)
     mapped_copy.start()
 
-    for axis in (1, 2, 0):
-        start, end, ssem, rsem = grad_ends(axis)
-        wait_in("py", end, ssem, rsem)
-
     last_rows[...] = jnp.zeros_like(last_rows)
-    for axis in range(3):
-
-        def add_up(c, carry):
-            rows = pl.ds(pl.multiple_of(32 * c, 32), 32)
-            total = grad_in[axis, 0, rows, :].astype(F32)
-            for s in range(1, PARTS):
-                total = total + grad_in[axis, s, rows, :].astype(F32)
-            for h in range(2):
-                last_rows[pl.ds(8 * axis + 2 * c + h, PARTS, stride=32), :] = total[16 * h : 16 * h + 16]
-            return carry
-
-        lax.fori_loop(0, 4, add_up, 0)
+
+    def collect(size):
+        for axis in (1, 2, 0):
+            start, end, ssem, rsem = grad_ends(axis, size)
+            wait_in("py", end, ssem, rsem)
+
+            def add_up(c, carry):
+                rows = pl.ds(pl.multiple_of(32 * c, 32), 32)
+                total = grad_in[axis, 0, rows, :].astype(F32)
+                for s in range(1, PARTS):
+                    total = total + grad_in[axis, s, rows, :].astype(F32)
+                for h in range(2):
+                    half = total[16 * h : 16 * h + 16]
+                    if size == 64:
+                        last_rows[pl.ds(8 * axis + 4 * c + h, PARTS, stride=32), :] = half
+                        last_rows[pl.ds(8 * axis + 4 * c + 2 + h, PARTS, stride=32), :] = pltpu.roll(half, 96, 1)
+                    else:
+                        last_rows[pl.ds(8 * axis + 2 * c + h, PARTS, stride=32), :] = half
+                return carry
+
+            lax.fori_loop(0, size // 32, add_up, 0)
+
+    @pl.when(py < 8)
+    def _():
+        collect(64)
+
+    @pl.when(py >= 8)
+    def _():
+        collect(128)
 
     for j in range(PARTS):
         last_out[j] = last_rows[32 * j : 32 * j + 32, :].astype(BF16)
@@ -643,8 +679,18 @@
     for m in range(7):
         wait_out(KINDS[m], leaving(m), send_sems.at[m], recv_sems.at[m])
     for axis in range(3):
-        start, end, ssem, rsem = grad_ends(axis)
-        wait_out("py", start, ssem, rsem)
+
+        def sent(j, carry):
+            for size, here in ((64, j < 8), (128, j >= 8)):
+                start, end, ssem, rsem = grad_ends(axis, size)
+
+                @pl.when(jnp.logical_and(here, j != py))
+                def _():
+                    remote(start(j), start(j), ssem.at[j], rsem.at[j], (px, py)).wait_send()
+
+            return carry
+
+        lax.fori_loop(0, PARTS, sent, 0)
     wait_in("px", last_ends[1], lsend_sems, lrecv_sems)
     total = last_in[0].astype(F32)
     for s in range(1, PARTS):

time: 77.8 us -> 76.6 us (0.985)
  Pallas kernels: 77.1 us -> 75.8 us
    pallas_call x1, Pallas kernels: 75.3 us -> 74 us  [per_device(): pl.pallas_call(layer_kernel, out_shape=shapes, in_specs=[anywhere] * 3, o...]
where the time goes in v5:
time: 76.6 us; the launch traced here: 76.5 us
  Pallas kernels  75.8 us (99%)
    pallas_call x1, Pallas kernels, per_device(): pl.pallas_call(layer_kernel, out_shape=shapes, in_specs=[anywhere] * 3, o...  74 us
    pallas_call x1, Pallas kernels, per_device(): pl.pallas_call(hand_over_kernel, out_shape=shapes, in_specs=[anywhere] *...  1.79 us

profile of v5, /device:TPU:1, one launch (start us, length us, event | category | flops | bytes accessed | tf_op | source)
XLA Modules:
  0.0 76.5 jit_solution(16116437219063628887)
XLA Ops:
  0.6 74.0 %flow_layer.1 = (bf16[2,4,4,4096]{3,2,1,0:T(4,128)(2,1)}, bf16[2,4,4,4096]{3,2,1,0:T(4,128)(2,1)}, f32[3,4,4,64]{3,2,1,0:T(4,128)}) custom-call(bf16[2,4,4,4096]{3,2,1,0:T(4,128)(2,1)} %field_ref.1, bf16[2,4,4,4096]{3,2,1,0:T(4,128)(2,1)} %cot_ref.1, bf16[3,64,64,64]{3,2,1,0:T(8,128)(2,1)} %taps_ref.1), custom_call_target="tpu_custom_call" | custom-call | tf_op jit(solution)/shard_map/flow_layer/pallas_call | solution.py:735
  74.7 1.8 %hand_over.1 = (bf16[2,4,4,4096]{3,2,1,0:T(4,128)(2,1)}, bf16[2,4,4,4096]{3,2,1,0:T(4,128)(2,1)}, f32[3,4,4,64]{3,2,1,0:T(4,128)}) custom-call(bf16[2,4,4,4096]{3,2,1,0:T(4,128)(2,1)} %get-tuple-element.6.mapped_in, bf16[2,4,4,4096]{3,2,1,0:T(4,128)(2,1)} %get-tuple-element.7.gfield_in, f32[3,4,4,64]{3,2,1,0:T(4,128)} %get-tuple-element.8.gtaps_in), custom_call_target="tpu_custom_call" | custom-call | tf_op jit(solution)/shard_map/hand_over/pallas_call | solution.py:779
